TPU v7x, 32 devices: a whole 2x2x4 slice. The times are simulated.
32 devices in a mesh: dp: 4 (over y, x), expert: 8 (over z, core).
Axes of the slice: x: 2, y: 2, z: 4, core: 2. Of those that a mesh axis runs over, the one named last changes fastest.
Arguments:
- tokens: bfloat16 [1024, 2048], P(('dp', 'expert')), may hold values from -6 to 6
- tangent: bfloat16 [1024, 2048], P(('dp', 'expert')), may hold values from -6 to 6
- norm_gain: float32 [2048], replicated, may hold values from 0.1 to 1.9
- router: bfloat16 [2048, 16], replicated, may hold values from -0.125 to 0.125
- w_gate: bfloat16 [16, 2048, 768], P('expert', 'dp'), may hold values from -0.125 to 0.125
- w_up: bfloat16 [16, 2048, 768], P('expert', 'dp'), may hold values from -0.125 to 0.125
- w_down: bfloat16 [16, 768, 2048], P('expert', None, 'dp'), may hold values from -0.21875 to 0.21875
- routes: int32 [1024, 8], P(('dp', 'expert')), may hold values from 0 to 15, all different within a row; in each aligned block of 32 rows (0 to 31, 32 to 63, ...) at most 32 rows name the same one
Outputs:
- tangent_image: float32 [1024, 2048], P(('dp', 'expert'))
- gram_image: float32 [1024, 2048], P(('dp', 'expert'))
Inputs may be any that keep to these rules, and one draw needn't show every extreme that they name: `routes`: each row names 8 different experts. Within the rows of one device (aligned blocks of 32 rows) no expert is named more than 32 times, and in some such blocks an expert is named exactly 32 times.
All inputs are finite; a program needn't handle non-finite values.
Results may differ from a plain program's by a relative error of at most 0.013.
Values may be sent and summed in bfloat16 or wider, within the bound.
A program may use at most 128 MiB of HBM per device.

v0:
```python
import jax
import jax.numpy as jnp
from jax import lax
from jax.experimental import pallas as pl
from jax.experimental.pallas import tpu as pltpu
from jax.sharding import PartitionSpec as P

eps_value = 1e-06


def pick_columns(table, routes):
    hits = routes[:, :, None] == jnp.arange(table.shape[1], dtype=jnp.int32)[None, None, :]
    return jnp.sum(jnp.where(hits, table[:, None, :], jnp.zeros((), table.dtype)), axis=2)


def on_device(tokens, tangent, norm_gain, router, w_gate, w_up, w_down, routes):
    tok_rows, topk = routes.shape
    model_width = tokens.shape[1]
    experts_all = router.shape[1]
    local_experts = w_gate.shape[0]
    groups = lax.axis_size("expert")
    capacity = 2 * tok_rows * topk // experts_all
    xfull = tokens.astype(jnp.float32)
    vfull = tangent.astype(jnp.float32)
    inv_rms = lax.rsqrt(jnp.mean(xfull * xfull, axis=1, keepdims=True) + eps_value)
    normed = (norm_gain * xfull * inv_rms).astype(jnp.bfloat16)
    cross_term = jnp.mean(xfull * vfull, axis=1, keepdims=True)
    normed_tan = (norm_gain * (vfull * inv_rms - xfull * inv_rms**3 * cross_term)).astype(
        jnp.bfloat16
    )
    logits = jnp.dot(normed, router, preferred_element_type=jnp.float32)
    logit_tan = jnp.dot(normed_tan, router, preferred_element_type=jnp.float32)
    selected = pick_columns(logits, routes)
    sel_tan = pick_columns(logit_tan, routes)
    exp_sel = jnp.exp(selected)
    gate_prob = exp_sel / jnp.sum(exp_sel, axis=1, keepdims=True)
    gate_tan = gate_prob * (sel_tan - jnp.sum(gate_prob * sel_tan, axis=1, keepdims=True))
    gate_b = gate_prob.astype(jnp.bfloat16)
    gate_tan_b = gate_tan.astype(jnp.bfloat16)
    pair_count = tok_rows * topk
    flat_ids = routes.reshape(-1)
    order = jnp.arange(pair_count, dtype=jnp.int32)
    earlier = (flat_ids[None, :] == flat_ids[:, None]) & (order[None, :] < order[:, None])
    slot_rank = jnp.sum(earlier.astype(jnp.int32), axis=1)
    slot_of_pair = flat_ids * capacity + slot_rank
    slot_hits = slot_of_pair[None, :] == jnp.arange(experts_all * capacity, dtype=jnp.int32)[:, None]
    slot_table = jnp.max(
        jnp.where(slot_hits, jnp.arange(pair_count, dtype=jnp.int32)[None, :], -1), axis=1
    )
    slot_valid = slot_table >= 0
    safe_pair = jnp.maximum(slot_table, 0)
    tok_idx = safe_pair // topk
    which_k = safe_pair % topk
    bf_zero = jnp.zeros((), jnp.bfloat16)
    send_rows = jnp.stack(
        (
            jnp.where(slot_valid[:, None], normed[tok_idx], bf_zero),
            jnp.where(slot_valid[:, None], normed_tan[tok_idx], bf_zero),
        )
    )
    send_rows = send_rows.reshape(2, groups, local_experts * capacity, model_width)
    send_gates = jnp.stack(
        (
            jnp.where(slot_valid, gate_b[tok_idx, which_k], bf_zero),
            jnp.where(slot_valid, gate_tan_b[tok_idx, which_k], bf_zero),
        )
    )
    send_gates = send_gates.reshape(2, groups, local_experts * capacity)
    recv_rows, recv_gates = (
        lax.all_to_all(send_rows, "expert", split_axis=1, concat_axis=1, tiled=True),
        lax.all_to_all(send_gates, "expert", split_axis=1, concat_axis=1, tiled=True),
    )
    slot_rows = recv_rows.reshape(2, groups, local_experts, capacity, model_width)
    recv_gates = recv_gates.reshape(2, groups, local_experts, capacity).astype(jnp.float32)
    gate_val = recv_gates[0][..., None]
    tan_val = recv_gates[1][..., None]
    gate_full, up_full, down_full = (
        lax.all_gather(w_gate, "dp", axis=1, tiled=True),
        lax.all_gather(w_up, "dp", axis=1, tiled=True),
        lax.all_gather(w_down, "dp", axis=2, tiled=True),
    )
    pre_both = jnp.einsum(
        "tslkd,ldf->tslkf", slot_rows, gate_full, preferred_element_type=jnp.float32
    )
    up_both = jnp.einsum("tslkd,ldf->tslkf", slot_rows, up_full, preferred_element_type=jnp.float32)
    pre_gate = pre_both[0]
    gate_dot = pre_both[1]
    pre_up = up_both[0]
    up_dot = up_both[1]
    sig_gate = jax.nn.sigmoid(pre_gate)
    silu_gate = pre_gate * sig_gate
    slope_gate = sig_gate * (1.0 + pre_gate * (1.0 - sig_gate))
    hidden = silu_gate * pre_up
    hidden_tan = slope_gate * gate_dot * pre_up + silu_gate * up_dot
    mixed_rows = (tan_val * hidden + gate_val * hidden_tan).astype(jnp.bfloat16)
    pair_image = jnp.einsum(
        "slkf,lfd->slkd", mixed_rows, down_full, preferred_element_type=jnp.float32
    )
    pair_send = pair_image.astype(jnp.bfloat16).reshape(
        groups, local_experts * capacity, model_width
    )
    pair_back = lax.all_to_all(pair_send, "expert", split_axis=0, concat_axis=0, tiled=True)
    pair_back = pair_back.reshape(experts_all * capacity, model_width)
    tangent_image = jnp.sum(
        pair_back[slot_of_pair].astype(jnp.float32).reshape(tok_rows, topk, model_width), axis=1
    )
    image_b = tangent_image.astype(jnp.bfloat16)
    send_cot = jnp.where(slot_valid[:, None], image_b[tok_idx], bf_zero).reshape(
        groups, local_experts * capacity, model_width
    )
    recv_cot = lax.all_to_all(send_cot, "expert", split_axis=0, concat_axis=0, tiled=True)
    recv_cot = recv_cot.reshape(groups, local_experts, capacity, model_width)
    back_hidden = jnp.einsum(
        "slkd,lfd->slkf", recv_cot, down_full, preferred_element_type=jnp.float32
    )
    gate_cot = jnp.sum(back_hidden * hidden, axis=3).astype(jnp.bfloat16)
    scaled = gate_val * back_hidden
    grad_gate = (scaled * pre_up * slope_gate).astype(jnp.bfloat16)
    grad_up = (scaled * silu_gate).astype(jnp.bfloat16)
    pair_grad = jnp.einsum(
        "slkf,ldf->slkd", grad_gate, gate_full, preferred_element_type=jnp.float32
    )
    pair_grad = pair_grad + jnp.einsum(
        "slkf,ldf->slkd", grad_up, up_full, preferred_element_type=jnp.float32
    )
    grad_send = pair_grad.astype(jnp.bfloat16).reshape(
        groups, local_experts * capacity, model_width
    )
    cot_send = gate_cot.reshape(groups, local_experts * capacity)
    grad_back, cot_back = (
        lax.all_to_all(grad_send, "expert", split_axis=0, concat_axis=0, tiled=True),
        lax.all_to_all(cot_send, "expert", split_axis=0, concat_axis=0, tiled=True),
    )
    grad_back = grad_back.reshape(experts_all * capacity, model_width)
    cot_back = cot_back.reshape(experts_all * capacity)
    expert_grad = jnp.sum(
        grad_back[slot_of_pair].astype(jnp.float32).reshape(tok_rows, topk, model_width), axis=1
    )
    pair_cot = cot_back[slot_of_pair].astype(jnp.float32).reshape(tok_rows, topk)
    logit_grad = gate_prob * (pair_cot - jnp.sum(gate_prob * pair_cot, axis=1, keepdims=True))
    hits = routes[:, :, None] == jnp.arange(experts_all, dtype=jnp.int32)[None, None, :]
    column_grad = jnp.sum(jnp.where(hits, logit_grad[:, :, None], 0.0), axis=1)
    router_grad = jnp.dot(
        column_grad, router.astype(jnp.float32).T, precision=lax.Precision.HIGHEST
    )
    pulled = norm_gain * (expert_grad + router_grad)
    gram_image = inv_rms * pulled - xfull * inv_rms**3 * jnp.mean(
        pulled * xfull, axis=1, keepdims=True
    )
    return (tangent_image, gram_image)


MESH = pl.DeviceIdType.MESH


def nt_dot(left, right):
    return lax.dot_general(
        left, right, (((1,), (1,)), ((), ())), preferred_element_type=jnp.float32
    )


def block_kernel(
    tok_ref, tan_ref, gain_ref, router_ref, routes_ref, wg_ref, wu_ref, wd_ref,
    image_ref, gram_ref,
    wgu, wd, rows, pre, mix, part, cross, summed, far, landed, image_rows,
    grads, part2, cross2, summed2, far2, landed2, prob_keep, inv_keep,
    w_send, w_recv, w_own, a_send, a_recv, r_send, r_recv, c_send, c_recv,
):
    f32, bf = jnp.float32, jnp.bfloat16
    n_tok, width = tok_ref.shape
    slab, hid = wg_ref.shape[1], wg_ref.shape[2]
    half = hid // 2
    n_core = 4 * n_tok
    dp, ex = lax.axis_index("dp"), lax.axis_index("expert")
    y, x = dp // 2, dp % 2
    z, core = ex // 2, ex % 2
    other = 1 - core
    x_peer = (y * 2 + 1 - x, ex)
    y_peer = ((1 - y) * 2 + x, ex)
    mate = (dp, z * 2 + other)
    z_peers = [(dp, (z + dz) % 4 * 2 + core) for dz in range(1, 4)]
    core_rows = pl.ds(pl.multiple_of(core * n_core, n_core), n_core)
    other_rows = pl.ds(pl.multiple_of(other * n_core, n_core), n_core)

    def block_rows(dz):
        return pl.ds(pl.multiple_of(core * n_core + (z + dz) % 4 * n_tok, n_tok), n_tok)

    def z_rows(dz):
        return pl.ds(pl.multiple_of((z + dz) % 4 * n_tok, n_tok), n_tok)

    slot_rows = block_rows(0)

    barrier = pltpu.get_barrier_semaphore()
    friends = z_peers + [x_peer, y_peer, mate]
    for friend in friends:
        pl.semaphore_signal(barrier, inc=1, device_id=friend, device_id_type=MESH)
    pl.semaphore_wait(barrier, len(friends))

    pending = []

    def push(src, dst, sems, where, device):
        copy = pltpu.make_async_remote_copy(
            src_ref=src, dst_ref=dst, send_sem=sems[0].at[where], recv_sem=sems[1].at[where],
            device_id=device, device_id_type=MESH,
        )
        copy.start()
        pending.append(copy)
        return copy

    def slab_of(index):
        return pl.ds(pl.multiple_of(index * slab, slab), slab)

    def weight_dst(kind, l, index):
        if kind == 2:
            return wd.at[pl.ds(l * half, half), slab_of(index)]
        return wgu.at[l, slab_of(index), pl.ds(kind * half, half)]

    def weight_src(kind, l, which):
        part_of = pl.ds(pl.multiple_of(which * half, half), half)
        if kind == 2:
            return wd_ref.at[l, part_of, :]
        return (wg_ref, wu_ref)[kind].at[l, :, part_of]

    moving, relayed = {}, {}
    w_sems = (w_send, w_recv)

    def start_weights(kind, l):
        mine = weight_dst(kind, l, dp)
        for_x, for_y = (1 - x, x) if l == 0 else (y, 1 - y)
        own = pltpu.make_async_copy(
            weight_src(kind, l, x if l == 0 else y), mine, w_own.at[kind, l]
        )
        ends = [(for_x, 0, x_peer), (for_y, 1, y_peer)]
        copies = [
            push(weight_src(kind, l, which), mine, w_sems, (kind, l, p), peer)
            for which, p, peer in ends
        ]
        own.start()
        moving[kind, l] = (copies, own)

    def relay_weights(kind, l):
        moving[kind, l][0][l].wait_recv()
        if l == 0:
            block = weight_dst(kind, l, y * 2 + 1 - x)
            relayed[kind, l] = push(block, block, w_sems, (kind, l, 2), y_peer)
        else:
            block = weight_dst(kind, l, (1 - y) * 2 + x)
            relayed[kind, l] = push(block, block, w_sems, (kind, l, 2), x_peer)

    def need_weights(kind, l):
        copies, own = moving[kind, l]
        own.wait()
        copies[1 - l].wait_recv()
        relayed[kind, l].wait_recv()

    a_sems, c_sems, r_sems = (a_send, a_recv), (c_send, c_recv), (r_send, r_recv)

    def gather_start(buf, turn):
        mine = buf.at[0, slot_rows]
        along_z = [
            push(mine, mine, a_sems, (turn, 0, i + 1), peer) for i, peer in enumerate(z_peers)
        ]
        sides = [
            {0: push(mine, buf.at[1 + s, slot_rows], a_sems, (turn, 1 + s, 0), peer)}
            for s, peer in enumerate((x_peer, y_peer))
        ]
        return along_z, sides, [push(mine, mine, c_sems, (turn, 0), mate)]

    def gather_finish(buf, turn, started):
        along_z, sides, to_mate = started
        for dz in (3, 1, 2):
            along_z[dz - 1].wait_recv()
            got = block_rows(4 - dz)
            block = buf.at[0, got]
            for s, peer in enumerate((x_peer, y_peer)):
                sides[s][dz] = push(
                    block, buf.at[1 + s, got], a_sems, (turn, 1 + s, dz), peer
                )
            to_mate.append(push(block, block, c_sems, (turn, dz), mate))
        for dz in (0, 3, 1, 2):
            for s in range(2):
                sides[s][dz].wait_recv()
                block = buf.at[1 + s, block_rows((4 - dz) % 4)]
                to_mate.append(push(block, block, c_sems, (turn, 4 + 4 * s + dz), mate))
        return to_mate

    def send_home(compute, parts, crossed, mid, far, land, turn):
        over, aside = {}, {}

        def to_mate(g):
            over[g] = push(
                parts.at[g, other_rows], crossed.at[g], c_sems, (2 + turn, g), mate
            )

        def add_mate(g):
            over[g].wait_recv()
            mid[g] = (parts[g, core_rows, :].astype(f32) + crossed[g].astype(f32)).astype(bf)

        def to_side(g, peer):
            add_mate(g)
            for dz in (2, 1, 3, 0):
                aside[g, dz] = push(
                    mid.at[g, z_rows(dz)], far.at[g - 1, z_rows(dz)],
                    r_sems, (turn, 4 * g + dz), peer,
                )

        compute(1)
        to_mate(1)
        compute(2)
        to_mate(2)
        to_side(1, x_peer)
        to_side(2, y_peer)
        compute(0)
        to_mate(0)
        over[0].wait_recv()
        copies = {}
        for dz in (2, 1, 3, 0):
            aside[1, dz].wait_recv()
            aside[2, dz].wait_recv()
            at = z_rows(dz)
            own = parts[0, block_rows(dz), :].astype(f32) + crossed[0, at, :].astype(f32)
            total = own + (far[0, at, :].astype(f32) + far[1, at, :].astype(f32))
            if dz:
                mid[0, at, :] = total.astype(bf)
                copies[dz] = push(
                    mid.at[0, at], land.at[z], r_sems, (turn, dz), z_peers[dz - 1]
                )
        for dz in (1, 3, 2):
            copies[dz].wait_recv()
            total = total + land[(z + 4 - dz) % 4].astype(f32)
        return total

    start_weights(0, 0)

    xfull = tok_ref[...].astype(f32)
    vfull = tan_ref[...].astype(f32)
    gain = gain_ref[...]
    inv_rms = lax.rsqrt(jnp.mean(xfull * xfull, axis=1, keepdims=True) + eps_value)
    normed = (gain * xfull * inv_rms).astype(bf)
    cross_term = jnp.mean(xfull * vfull, axis=1, keepdims=True)
    inv_cube = inv_rms * inv_rms * inv_rms
    normed_tan = (gain * (vfull * inv_rms - xfull * inv_cube * cross_term)).astype(bf)
    rows[0, slot_rows, 0:width] = normed
    rows[0, slot_rows, width : 2 * width] = normed_tan
    logits = jnp.dot(normed, router_ref[...], preferred_element_type=f32)
    logit_tan = jnp.dot(normed_tan, router_ref[...], preferred_element_type=f32)
    lanes = lax.broadcasted_iota(jnp.int32, (n_tok, 128), 1)
    chosen = jnp.zeros((n_tok, 128), f32)
    for k in range(routes_ref.shape[1]):
        chosen = chosen + jnp.where(lanes == routes_ref[:, k : k + 1], 1.0, 0.0)
    exp_sel = jnp.where(chosen > 0.5, jnp.exp(logits), 0.0)
    gate_prob = exp_sel / jnp.sum(exp_sel, axis=1, keepdims=True)
    gate_tan = gate_prob * (
        logit_tan - jnp.sum(gate_prob * logit_tan, axis=1, keepdims=True)
    )
    rows[0, slot_rows, 2 * width : 2 * width + 128] = gate_prob.astype(bf)
    rows[0, slot_rows, 2 * width + 128 : 2 * width + 256] = gate_tan.astype(bf)
    prob_keep[...] = gate_prob
    inv_keep[...] = jnp.broadcast_to(inv_rms, (n_tok, 128))

    started = gather_start(rows, 0)
    pieces = [(0, 0), (1, 0), (0, 1), (1, 1), (2, 0), (2, 1)]
    for kind, l in pieces[1:]:
        start_weights(kind, l)
    for copy in gather_finish(rows, 0, started):
        copy.wait_recv()
    for kind, l in pieces:
        relay_weights(kind, l)

    n_rows = rows.shape[1]
    wide_lanes = lax.broadcasted_iota(jnp.int32, (n_rows, 128), 1)

    def gate_of(part_no, l, offset):
        table = rows[part_no, :, 2 * width + offset : 2 * width + offset + 128].astype(f32)
        return jnp.sum(jnp.where(wide_lanes == ex * 2 + l, table, 0.0), axis=1, keepdims=True)

    for l in range(2):
        need_weights(0, l)
        need_weights(1, l)

        @pl.loop(0, 2)
        def _(h):
            g = h * (l + 1)
            pre[l, h] = jnp.dot(rows[g, :, 0:width], wgu[l], preferred_element_type=f32)
            dots = jnp.dot(rows[g, :, width : 2 * width], wgu[l], preferred_element_type=f32)
            pre_gate, pre_up = pre[l, h, :, 0:half], pre[l, h, :, half:hid]
            gate_dot, up_dot = dots[:, 0:half], dots[:, half:hid]
            sig = jax.nn.sigmoid(pre_gate)
            silu = pre_gate * sig
            slope = sig * (1.0 + pre_gate * (1.0 - sig))
            hidden_tan = slope * gate_dot * pre_up + silu * up_dot
            mixed = gate_of(g, l, 128) * (silu * pre_up) + gate_of(g, l, 0) * hidden_tan
            mix[g, :, l * half : (l + 1) * half] = mixed.astype(bf)

    need_weights(2, 0)
    need_weights(2, 1)

    spans = [(0, hid), (0, half), (half, hid)]

    def down(g):
        lo, hi = spans[g]
        part[g] = jnp.dot(mix[g, :, lo:hi], wd[lo:hi, :], preferred_element_type=f32).astype(bf)

    image = send_home(down, part, cross, summed, far, landed, 0)
    image_ref[...] = image
    image_rows[0, slot_rows, :] = image.astype(bf)
    for copy in gather_finish(image_rows, 1, gather_start(image_rows, 1)):
        copy.wait_recv()

    def backward(g):
        lo, hi = spans[g]
        back = nt_dot(image_rows[g], wd[lo:hi, :])
        cots = jnp.zeros((n_rows, 128), f32)
        total = None
        for l in range(lo // half, hi // half):
            back_hidden = back[:, l * half - lo : (l + 1) * half - lo]
            h = 1 if g else 0
            pre_gate, pre_up = pre[l, h, :, 0:half], pre[l, h, :, half:hid]
            sig = jax.nn.sigmoid(pre_gate)
            silu = pre_gate * sig
            slope = sig * (1.0 + pre_gate * (1.0 - sig))
            cot = jnp.sum(back_hidden * (silu * pre_up), axis=1, keepdims=True)
            cots = cots + jnp.where(wide_lanes == ex * 2 + l, cot, 0.0)
            scaled = gate_of(g, l, 0) * back_hidden
            grads[l, :, 0:half] = (scaled * pre_up * slope).astype(bf)
            grads[l, :, half:hid] = (scaled * silu).astype(bf)
            term = nt_dot(grads[l], wgu[l])
            total = term if total is None else total + term
        part2[g, :, 0:width] = total.astype(bf)
        part2[g, :, width : width + 128] = cots.astype(bf)

    total = send_home(backward, part2, cross2, summed2, far2, landed2, 1)

    expert_grad = total[:, 0:width]
    cot = total[:, width : width + 128]
    prob = prob_keep[...]
    column_grad = prob * (cot - jnp.sum(prob * cot, axis=1, keepdims=True))
    high = column_grad.astype(bf)
    rest = column_grad - high.astype(f32)
    middle = rest.astype(bf)
    low = (rest - middle.astype(f32)).astype(bf)
    router = router_ref[...]
    router_grad = nt_dot(high, router) + (nt_dot(middle, router) + nt_dot(low, router))
    xfull = tok_ref[...].astype(f32)
    inv_rms = inv_keep[:, 0:1]
    pulled = gain_ref[...] * (expert_grad + router_grad)
    gram_ref[...] = inv_rms * pulled - xfull * (inv_rms * inv_rms * inv_rms) * jnp.mean(
        pulled * xfull, axis=1, keepdims=True
    )
    for copy in pending:
        copy.wait_send()


def on_device_dense(tokens, tangent, norm_gain, router, w_gate, w_up, w_down, routes):
    n_tok, width = tokens.shape
    hid = w_gate.shape[2]
    n_rows = 8 * n_tok
    bf, f32 = jnp.bfloat16, jnp.float32
    wide_router = jnp.pad(router, ((0, 0), (0, 128 - router.shape[1])))
    vm = pl.BlockSpec(memory_space=pltpu.VMEM)
    hbm = pl.BlockSpec(memory_space=pl.ANY)
    out = jax.ShapeDtypeStruct((n_tok, width), f32)
    dma = pltpu.SemaphoreType.DMA
    image, gram = pl.pallas_call(
        block_kernel,
        out_shape=(out, out),
        in_specs=[vm] * 5 + [hbm] * 3,
        out_specs=(vm, vm),
        scratch_shapes=[
            pltpu.VMEM((2, width, hid), bf),
            pltpu.VMEM((hid, width), bf),
            pltpu.VMEM((3, n_rows, 2 * width + 256), bf),
            pltpu.VMEM((2, 2, n_rows, hid), f32),
            pltpu.VMEM((3, n_rows, hid), bf),
            pltpu.VMEM((3, n_rows, width), bf),
            pltpu.VMEM((3, n_rows // 2, width), bf),
            pltpu.VMEM((3, n_rows // 2, width), bf),
            pltpu.VMEM((2, n_rows // 2, width), bf),
            pltpu.VMEM((4, n_tok, width), bf),
            pltpu.VMEM((3, n_rows, width), bf),
            pltpu.VMEM((2, n_rows, hid), bf),
            pltpu.VMEM((3, n_rows, width + 128), bf),
            pltpu.VMEM((3, n_rows // 2, width + 128), bf),
            pltpu.VMEM((3, n_rows // 2, width + 128), bf),
            pltpu.VMEM((2, n_rows // 2, width + 128), bf),
            pltpu.VMEM((4, n_tok, width + 128), bf),
            pltpu.VMEM((n_tok, 128), f32),
            pltpu.VMEM((n_tok, 128), f32),
            dma((3, 2, 3)), dma((3, 2, 3)), dma((3, 2)),
            dma((2, 3, 4)), dma((2, 3, 4)), dma((2, 12)), dma((2, 12)), dma((4, 12)), dma((4, 12)),
        ],
        compiler_params=pltpu.CompilerParams(
            collective_id=0, has_side_effects=True, vmem_limit_bytes=60 * 2**20
        ),
        cost_estimate=pl.CostEstimate(
            flops=2 * 16 * n_rows * width * hid, bytes_accessed=2**24, transcendentals=2**20
        ),
    )(tokens, tangent, norm_gain.reshape(1, width), wide_router, routes, w_gate, w_up, w_down)
    return image, gram


def solution(mesh):
    in_specs = (
        P(("dp", "expert"), None),
        P(("dp", "expert"), None),
        P(),
        P(),
        P("expert", "dp", None),
        P("expert", "dp", None),
        P("expert", None, "dp"),
        P(("dp", "expert"), None),
    )
    out_specs = (P(("dp", "expert"), None), P(("dp", "expert"), None))
    body = on_device
    if mesh.shape["dp"] == 4 and mesh.shape["expert"] == 8:
        body = on_device_dense
    return jax.shard_map(
        body, mesh=mesh, in_specs=in_specs, out_specs=out_specs, check_vma=False
    )
```

profile of v0, /device:TPU:0, one launch (start us, length us, event | category | flops | bytes accessed | tf_op | source)
XLA Modules:
  0.0 186.2 jit_solution(4533454249391273098)
XLA Ops:
  0.6 1.4 copy.11.routes_ref
  2.0 1.1 copy.10
  3.1 0.9 pad.4.router_ref
  4.0 178.8 %shard_map.95 = (f32[32,2048]{1,0:T(8,128)}, f32[32,2048]{1,0:T(8,128)}) custom-call(bf16[32,2048]{1,0:T(8,128)(2,1)} %tok_ref.1, bf16[32,2048]{1,0:T(8,128)(2,1)} %tan_ref.1, f32[1,2048]{1,0:T(1,128)} %bitcast.1, bf16[2048,128]{1,0:T(8,128)(2,1)} %pad.4.router_ref, s32[32,8]{1,0:T(8,128)} %copy.11.routes_ref, bf16[2,512,768]{2,1,0:T(8,128)(2,1)} %wg_ref.1, ...), custom_call_target="tpu_custom_call" | custom-call | flops 12884901888 | bytes 16777216 | tf_op jit(solution)/shard_map/pallas_call | solution.py:464
  182.8 1.7 copy.14
  184.5 1.7 copy.15
where the time goes:
time: 186 us
  Pallas kernels  179 us (96%)
  local copies, waits for them, and re-layouts  6.71 us (4%)
    pallas_call x1, Pallas kernels, on_device_dense(): pl.pallas_call(block_kernel, out_shape=(out, out), in_specs=[vm] * 5 + [h...  179 us
    unnamed x4, local copies, waits for them, and re-layouts  5.82 us

commit v1 on v0

v1 whole, which is shorter than its diff:
```python
import jax
import jax.numpy as jnp
from jax import lax
from jax.experimental import pallas as pl
from jax.experimental.pallas import tpu as pltpu
from jax.sharding import PartitionSpec as P

eps_value = 1e-06


def pick_columns(table, routes):
    hits = routes[:, :, None] == jnp.arange(table.shape[1], dtype=jnp.int32)[None, None, :]
    return jnp.sum(jnp.where(hits, table[:, None, :], jnp.zeros((), table.dtype)), axis=2)


def on_device(tokens, tangent, norm_gain, router, w_gate, w_up, w_down, routes):
    tok_rows, topk = routes.shape
    model_width = tokens.shape[1]
    experts_all = router.shape[1]
    local_experts = w_gate.shape[0]
    groups = lax.axis_size("expert")
    capacity = 2 * tok_rows * topk // experts_all
    xfull = tokens.astype(jnp.float32)
    vfull = tangent.astype(jnp.float32)
    inv_rms = lax.rsqrt(jnp.mean(xfull * xfull, axis=1, keepdims=True) + eps_value)
    normed = (norm_gain * xfull * inv_rms).astype(jnp.bfloat16)
    cross_term = jnp.mean(xfull * vfull, axis=1, keepdims=True)
    normed_tan = (norm_gain * (vfull * inv_rms - xfull * inv_rms**3 * cross_term)).astype(
        jnp.bfloat16
    )
    logits = jnp.dot(normed, router, preferred_element_type=jnp.float32)
    logit_tan = jnp.dot(normed_tan, router, preferred_element_type=jnp.float32)
    selected = pick_columns(logits, routes)
    sel_tan = pick_columns(logit_tan, routes)
    exp_sel = jnp.exp(selected)
    gate_prob = exp_sel / jnp.sum(exp_sel, axis=1, keepdims=True)
    gate_tan = gate_prob * (sel_tan - jnp.sum(gate_prob * sel_tan, axis=1, keepdims=True))
    gate_b = gate_prob.astype(jnp.bfloat16)
    gate_tan_b = gate_tan.astype(jnp.bfloat16)
    pair_count = tok_rows * topk
    flat_ids = routes.reshape(-1)
    order = jnp.arange(pair_count, dtype=jnp.int32)
    earlier = (flat_ids[None, :] == flat_ids[:, None]) & (order[None, :] < order[:, None])
    slot_rank = jnp.sum(earlier.astype(jnp.int32), axis=1)
    slot_of_pair = flat_ids * capacity + slot_rank
    slot_hits = slot_of_pair[None, :] == jnp.arange(experts_all * capacity, dtype=jnp.int32)[:, None]
    slot_table = jnp.max(
        jnp.where(slot_hits, jnp.arange(pair_count, dtype=jnp.int32)[None, :], -1), axis=1
    )
    slot_valid = slot_table >= 0
    safe_pair = jnp.maximum(slot_table, 0)
    tok_idx = safe_pair // topk
    which_k = safe_pair % topk
    bf_zero = jnp.zeros((), jnp.bfloat16)
    send_rows = jnp.stack(
        (
            jnp.where(slot_valid[:, None], normed[tok_idx], bf_zero),
            jnp.where(slot_valid[:, None], normed_tan[tok_idx], bf_zero),
        )
    )
    send_rows = send_rows.reshape(2, groups, local_experts * capacity, model_width)
    send_gates = jnp.stack(
        (
            jnp.where(slot_valid, gate_b[tok_idx, which_k], bf_zero),
            jnp.where(slot_valid, gate_tan_b[tok_idx, which_k], bf_zero),
        )
    )
    send_gates = send_gates.reshape(2, groups, local_experts * capacity)
    recv_rows, recv_gates = (
        lax.all_to_all(send_rows, "expert", split_axis=1, concat_axis=1, tiled=True),
        lax.all_to_all(send_gates, "expert", split_axis=1, concat_axis=1, tiled=True),
    )
    slot_rows = recv_rows.reshape(2, groups, local_experts, capacity, model_width)
    recv_gates = recv_gates.reshape(2, groups, local_experts, capacity).astype(jnp.float32)
    gate_val = recv_gates[0][..., None]
    tan_val = recv_gates[1][..., None]
    gate_full, up_full, down_full = (
        lax.all_gather(w_gate, "dp", axis=1, tiled=True),
        lax.all_gather(w_up, "dp", axis=1, tiled=True),
        lax.all_gather(w_down, "dp", axis=2, tiled=True),
    )
    pre_both = jnp.einsum(
        "tslkd,ldf->tslkf", slot_rows, gate_full, preferred_element_type=jnp.float32
    )
    up_both = jnp.einsum("tslkd,ldf->tslkf", slot_rows, up_full, preferred_element_type=jnp.float32)
    pre_gate = pre_both[0]
    gate_dot = pre_both[1]
    pre_up = up_both[0]
    up_dot = up_both[1]
    sig_gate = jax.nn.sigmoid(pre_gate)
    silu_gate = pre_gate * sig_gate
    slope_gate = sig_gate * (1.0 + pre_gate * (1.0 - sig_gate))
    hidden = silu_gate * pre_up
    hidden_tan = slope_gate * gate_dot * pre_up + silu_gate * up_dot
    mixed_rows = (tan_val * hidden + gate_val * hidden_tan).astype(jnp.bfloat16)
    pair_image = jnp.einsum(
        "slkf,lfd->slkd", mixed_rows, down_full, preferred_element_type=jnp.float32
    )
    pair_send = pair_image.astype(jnp.bfloat16).reshape(
        groups, local_experts * capacity, model_width
    )
    pair_back = lax.all_to_all(pair_send, "expert", split_axis=0, concat_axis=0, tiled=True)
    pair_back = pair_back.reshape(experts_all * capacity, model_width)
    tangent_image = jnp.sum(
        pair_back[slot_of_pair].astype(jnp.float32).reshape(tok_rows, topk, model_width), axis=1
    )
    image_b = tangent_image.astype(jnp.bfloat16)
    send_cot = jnp.where(slot_valid[:, None], image_b[tok_idx], bf_zero).reshape(
        groups, local_experts * capacity, model_width
    )
    recv_cot = lax.all_to_all(send_cot, "expert", split_axis=0, concat_axis=0, tiled=True)
    recv_cot = recv_cot.reshape(groups, local_experts, capacity, model_width)
    back_hidden = jnp.einsum(
        "slkd,lfd->slkf", recv_cot, down_full, preferred_element_type=jnp.float32
    )
    gate_cot = jnp.sum(back_hidden * hidden, axis=3).astype(jnp.bfloat16)
    scaled = gate_val * back_hidden
    grad_gate = (scaled * pre_up * slope_gate).astype(jnp.bfloat16)
    grad_up = (scaled * silu_gate).astype(jnp.bfloat16)
    pair_grad = jnp.einsum(
        "slkf,ldf->slkd", grad_gate, gate_full, preferred_element_type=jnp.float32
    )
    pair_grad = pair_grad + jnp.einsum(
        "slkf,ldf->slkd", grad_up, up_full, preferred_element_type=jnp.float32
    )
    grad_send = pair_grad.astype(jnp.bfloat16).reshape(
        groups, local_experts * capacity, model_width
    )
    cot_send = gate_cot.reshape(groups, local_experts * capacity)
    grad_back, cot_back = (
        lax.all_to_all(grad_send, "expert", split_axis=0, concat_axis=0, tiled=True),
        lax.all_to_all(cot_send, "expert", split_axis=0, concat_axis=0, tiled=True),
    )
    grad_back = grad_back.reshape(experts_all * capacity, model_width)
    cot_back = cot_back.reshape(experts_all * capacity)
    expert_grad = jnp.sum(
        grad_back[slot_of_pair].astype(jnp.float32).reshape(tok_rows, topk, model_width), axis=1
    )
    pair_cot = cot_back[slot_of_pair].astype(jnp.float32).reshape(tok_rows, topk)
    logit_grad = gate_prob * (pair_cot - jnp.sum(gate_prob * pair_cot, axis=1, keepdims=True))
    hits = routes[:, :, None] == jnp.arange(experts_all, dtype=jnp.int32)[None, None, :]
    column_grad = jnp.sum(jnp.where(hits, logit_grad[:, :, None], 0.0), axis=1)
    router_grad = jnp.dot(
        column_grad, router.astype(jnp.float32).T, precision=lax.Precision.HIGHEST
    )
    pulled = norm_gain * (expert_grad + router_grad)
    gram_image = inv_rms * pulled - xfull * inv_rms**3 * jnp.mean(
        pulled * xfull, axis=1, keepdims=True
    )
    return (tangent_image, gram_image)


MESH = pl.DeviceIdType.MESH


def nt_dot(left, right):
    return lax.dot_general(
        left, right, (((1,), (1,)), ((), ())), preferred_element_type=jnp.float32
    )


def nn_dot(left, right):
    return jnp.dot(left, right, preferred_element_type=jnp.float32)


def block_kernel(
    tok_ref, tan_ref, gain_ref, router_ref, routes_ref, wg_ref, wu_ref, wd_ref,
    image_ref, gram_ref,
    wgu, wd, rows, keep_a, keep_s, keep_h, mix, part, own_part, mid, far, landed,
    image_rows, grads, part2, own_part2, mid2, far2, landed2, prob_keep, inv_keep, router_pad,
    w_send, w_recv, w_own, m_send, m_recv, t_send, t_recv, a_send, a_recv, s_send, s_recv,
    z_send, z_recv,
):
    f32, bf = jnp.float32, jnp.bfloat16
    n_tok, width = tok_ref.shape
    slab, hid = wg_ref.shape[1], wg_ref.shape[2]
    half = hid // 2
    n_lane = 4 * n_tok
    n_exp = router_ref.shape[0]
    dp, ex = lax.axis_index("dp"), lax.axis_index("expert")
    y, x = dp // 2, dp % 2
    z, core = ex // 2, ex % 2
    x_index, y_index = y * 2 + 1 - x, (1 - y) * 2 + x
    d_index = (1 - y) * 2 + 1 - x
    x_peer, y_peer = (x_index, ex), (y_index, ex)
    mate = (dp, z * 2 + 1 - core)
    z_peers = [(dp, (z + dz) % 4 * 2 + core) for dz in range(1, 4)]
    at_x, at_own, at_y = 0, n_lane, 2 * n_lane

    def rows_of(base, dz):
        return pl.ds(pl.multiple_of(base + (z + dz) % 4 * n_tok, n_tok), n_tok)

    barrier = pltpu.get_barrier_semaphore()
    friends = z_peers + [x_peer, y_peer, mate]
    for friend in friends:
        pl.semaphore_signal(barrier, inc=1, device_id=friend, device_id_type=MESH)
    pl.semaphore_wait(barrier, len(friends))

    pending = []

    def push(src, dst, sems, where, device):
        copy = pltpu.make_async_remote_copy(
            src_ref=src, dst_ref=dst, send_sem=sems[0].at[where], recv_sem=sems[1].at[where],
            device_id=device, device_id_type=MESH,
        )
        copy.start()
        pending.append(copy)
        return copy

    def slab_of(index):
        return pl.ds(pl.multiple_of(index * slab, slab), slab)

    def weight_at(kind, l, index):
        if kind == 2:
            return wd.at[l, pl.ds(pl.multiple_of(core * half, half), half), slab_of(index)]
        first = pl.multiple_of(core * hid + kind * half, half)
        return wgu.at[l, slab_of(index), pl.ds(first, half)]

    def weight_src(kind, l, which):
        part_of = pl.ds(pl.multiple_of(which * half, half), half)
        if kind == 2:
            return wd_ref.at[l, part_of, :]
        return (wg_ref, wu_ref)[kind].at[l, :, part_of]

    direct, relayed, shared, local = {}, {}, {}, {}
    w_sems, m_sems, t_sems = (w_send, w_recv), (m_send, m_recv), (t_send, t_recv)
    a_sems, s_sems, z_sems = (a_send, a_recv), (s_send, s_recv), (z_send, z_recv)

    def start_weights(kind, l):
        mine = weight_at(kind, l, dp)
        for_x, for_y = (1 - x, x) if l == 0 else (y, 1 - y)
        for_me = x if l == 0 else y
        direct[kind, l] = [
            push(weight_src(kind, l, for_x), mine, w_sems, (kind, l, 0), x_peer),
            push(weight_src(kind, l, for_y), mine, w_sems, (kind, l, 1), y_peer),
        ]
        local[kind, l] = pltpu.make_async_copy(
            weight_src(kind, l, for_me), mine, w_own.at[kind, l]
        )
        local[kind, l].start()
        shared[kind, l] = [
            push(weight_src(kind, l, for_me), mine, m_sems, (kind, l, 0), mate)
        ]

    def share_weights(kind, l, slot, index):
        block = weight_at(kind, l, index)
        shared[kind, l].append(push(block, block, m_sems, (kind, l, slot), mate))

    def relay_weights(kind, l):
        block = weight_at(kind, l, (x_index, y_index)[l])
        direct[kind, l][l].wait_recv()
        relayed[kind, l] = push(block, block, w_sems, (kind, l, 2), (y_peer, x_peer)[l])
        share_weights(kind, l, 1, (x_index, y_index)[l])
        direct[kind, l][1 - l].wait_recv()
        share_weights(kind, l, 2, (x_index, y_index)[1 - l])

    def last_weights(kind, l):
        relayed[kind, l].wait_recv()
        share_weights(kind, l, 3, d_index)

    def need_weights(kind, l):
        local[kind, l].wait()
        for copy in shared[kind, l]:
            copy.wait_recv()

    start_weights(0, 0)

    router_pad[...] = jnp.zeros(router_pad.shape, bf)
    router_pad[0:n_exp, :] = router_ref[...]
    xfull = tok_ref[...].astype(f32)
    vfull = tan_ref[...].astype(f32)
    gain = gain_ref[...]
    inv_rms = lax.rsqrt(jnp.mean(xfull * xfull, axis=1, keepdims=True) + eps_value)
    normed = (gain * xfull * inv_rms).astype(bf)
    cross_term = jnp.mean(xfull * vfull, axis=1, keepdims=True)
    inv_cube = inv_rms * inv_rms * inv_rms
    normed_tan = (gain * (vfull * inv_rms - xfull * inv_cube * cross_term)).astype(bf)
    mine = rows_of(at_own, 0)
    rows[mine, 0:width] = normed
    rows[mine, width : 2 * width] = normed_tan
    logits = nt_dot(normed, router_pad[...])
    logit_tan = nt_dot(normed_tan, router_pad[...])
    ids = lax.broadcasted_iota(jnp.int32, (128, n_tok), 0)
    chosen_by = jnp.zeros((128, n_tok), f32)
    for k in range(routes_ref.shape[0]):
        chosen_by = chosen_by + jnp.where(ids == routes_ref[k : k + 1, :], 1.0, 0.0)
    unit = jnp.where(
        lax.broadcasted_iota(jnp.int32, (n_tok, n_tok), 0)
        == lax.broadcasted_iota(jnp.int32, (n_tok, n_tok), 1),
        1.0, 0.0,
    ).astype(bf)
    chosen = nt_dot(unit, chosen_by.astype(bf))
    exp_sel = jnp.where(chosen > 0.5, jnp.exp(logits), 0.0)
    gate_prob = exp_sel / jnp.sum(exp_sel, axis=1, keepdims=True)
    gate_tan = gate_prob * (
        logit_tan - jnp.sum(gate_prob * logit_tan, axis=1, keepdims=True)
    )
    rows[mine, 2 * width : 2 * width + 128] = (
        gate_prob + pltpu.roll(gate_tan, 64, 1)
    ).astype(bf)
    prob_keep[...] = gate_prob
    inv_keep[...] = jnp.broadcast_to(inv_rms, (n_tok, 128))

    def along_z(buf, base, sems, which):
        block = buf.at[rows_of(base, 0)]
        return [push(block, block, sems, (which, dz), z_peers[dz - 1]) for dz in (2, 1, 3)]

    from_x = push(rows.at[mine], rows.at[rows_of(at_x, 0)], t_sems, (0, 0), x_peer)
    from_y = push(rows.at[mine], rows.at[rows_of(at_y, 0)], t_sems, (2, 0), y_peer)
    token_copies = along_z(rows, at_own, t_sems, 1)
    pieces = [(0, 0), (1, 0), (0, 1), (1, 1), (2, 0), (2, 1)]
    for kind, l in pieces[1:]:
        start_weights(kind, l)
    from_x.wait_recv()
    token_copies += along_z(rows, at_x, t_sems, 0)
    from_y.wait_recv()
    token_copies += along_z(rows, at_y, t_sems, 2)
    for kind, l in pieces:
        relay_weights(kind, l)
    for kind, l in pieces[:4]:
        last_weights(kind, l)
    for copy in token_copies:
        copy.wait_recv()

    n_rows = 2 * n_lane
    wide_lanes = lax.broadcasted_iota(jnp.int32, (n_rows, 128), 1)

    for l in range(2):
        need_weights(0, l)
        need_weights(1, l)
        these = pl.ds(l * n_lane, n_rows)

        @pl.loop(0, 2)
        def _(k):
            cols = pl.ds(pl.multiple_of(k * hid, hid), hid)
            expert = (z * 2 + k) * 2 + l
            table = rows[these, 2 * width : 2 * width + 128].astype(f32)
            gate = jnp.sum(jnp.where(wide_lanes == expert, table, 0.0), axis=1, keepdims=True)
            tan = jnp.sum(
                jnp.where(wide_lanes == expert + 64, table, 0.0), axis=1, keepdims=True
            )
            pre = nn_dot(rows[these, 0:width], wgu[l, :, cols])
            dots = nn_dot(rows[these, width : 2 * width], wgu[l, :, cols])
            pre_gate, pre_up = pre[:, 0:half], pre[:, half:hid]
            gate_dot, up_dot = dots[:, 0:half], dots[:, half:hid]
            sig = jax.nn.sigmoid(pre_gate)
            silu = pre_gate * sig
            slope_up = sig * (1.0 + pre_gate * (1.0 - sig)) * pre_up
            hidden = silu * pre_up
            mixed = tan * hidden + gate * (slope_up * gate_dot + silu * up_dot)
            keep_a[l, k] = gate * slope_up
            keep_s[l, k] = gate * silu
            keep_h[l, k] = hidden
            mix[l, :, pl.ds(pl.multiple_of(k * half, half), half)] = mixed.astype(bf)

    for kind, l in pieces[4:]:
        last_weights(kind, l)

    def send_side(parts, far, turn, s):
        peer, base = ((x_peer, at_x), (y_peer, at_y))[s]
        return [
            push(
                parts.at[rows_of(base, dz)], far.at[s, rows_of(0, dz)],
                s_sems, (turn, s, dz), peer,
            )
            for dz in (2, 1, 3, 0)
        ]

    def send_home(compute, parts, own, mid, far, land, turn):
        compute(0)
        x_copies = send_side(parts, far, turn, 0)
        compute(1)
        y_copies = send_side(parts, far, turn, 1)
        copies = {}
        for i, dz in enumerate((2, 1, 3, 0)):
            x_copies[i].wait_recv()
            y_copies[i].wait_recv()
            at = rows_of(0, dz)
            total = own[at, :] + (far[0, at, :].astype(f32) + far[1, at, :].astype(f32))
            if dz:
                mid[dz] = total.astype(bf)
                copies[dz] = push(
                    mid.at[dz], land.at[z], z_sems, (turn, dz), z_peers[dz - 1]
                )
        for dz in (1, 3, 2):
            copies[dz].wait_recv()
            total = total + land[(z + 4 - dz) % 4].astype(f32)
        return total

    step = width // 4

    def place(parts, own, l, cols, term):
        if l == 0:
            parts[at_x : at_x + n_lane, cols] = term[0:n_lane].astype(bf)
            own[:, cols] = term[n_lane:n_rows]
        else:
            own[:, cols] = own[:, cols] + term[0:n_lane]
            parts[at_y : at_y + n_lane, cols] = term[n_lane:n_rows].astype(bf)

    def down(l):
        need_weights(2, l)

        @pl.loop(0, 4)
        def _(j):
            cols = pl.ds(pl.multiple_of(j * step, step), step)
            place(part, own_part, l, cols, nn_dot(mix[l], wd[l, :, cols]))

    image = send_home(down, part, own_part, mid, far, landed, 0)
    image_ref[...] = image
    image_rows[mine, :] = image.astype(bf)

    def gather_image():
        block = image_rows.at[mine]
        to_z = {dz: push(block, block, a_sems, (0, dz), z_peers[dz - 1]) for dz in (2, 1, 3)}
        sides = []

        def to_sides(dz):
            block = image_rows.at[rows_of(at_own, 4 - dz)]
            for s, (peer, base) in enumerate(((x_peer, at_x), (y_peer, at_y))):
                sides.append(
                    push(block, image_rows.at[rows_of(base, 4 - dz)], a_sems, (1 + s, dz), peer)
                )

        to_sides(0)
        for dz in (3, 1, 2):
            to_z[dz].wait_recv()
            to_sides(dz)
        for copy in sides:
            copy.wait_recv()

    gather_image()

    def backward(l):
        these = pl.ds(l * n_lane, n_rows)
        cots = jnp.zeros((n_rows, 128), f32)
        for k in range(2):
            back = nt_dot(image_rows[these, :], wd[l, k * half : (k + 1) * half, :])
            cot = jnp.sum(back * keep_h[l, k], axis=1, keepdims=True)
            cots = cots + jnp.where(wide_lanes == (z * 2 + k) * 2 + l, cot, 0.0)
            grads[l, :, k * hid : k * hid + half] = (back * keep_a[l, k]).astype(bf)
            grads[l, :, k * hid + half : (k + 1) * hid] = (back * keep_s[l, k]).astype(bf)
        place(part2, own_part2, l, slice(width, width + 128), cots)

        @pl.loop(0, 4)
        def _(j):
            cols = pl.ds(pl.multiple_of(j * step, step), step)
            place(part2, own_part2, l, cols, nt_dot(grads[l], wgu[l, cols, :]))

    total = send_home(backward, part2, own_part2, mid2, far2, landed2, 1)

    expert_grad = total[:, 0:width]
    cot = total[:, width : width + 128]
    prob = prob_keep[...]
    column_grad = prob * (cot - jnp.sum(prob * cot, axis=1, keepdims=True))
    high = column_grad.astype(bf)
    rest = column_grad - high.astype(f32)
    middle = rest.astype(bf)
    low = (rest - middle.astype(f32)).astype(bf)
    router = router_pad[...]
    router_grad = nn_dot(high, router) + (nn_dot(middle, router) + nn_dot(low, router))
    xfull = tok_ref[...].astype(f32)
    inv_rms = inv_keep[:, 0:1]
    pulled = gain_ref[...] * (expert_grad + router_grad)
    gram_ref[...] = inv_rms * pulled - xfull * (inv_rms * inv_rms * inv_rms) * jnp.mean(
        pulled * xfull, axis=1, keepdims=True
    )
    for copy in pending:
        copy.wait_send()


def on_device_dense(tokens, tangent, norm_gain, router, w_gate, w_up, w_down, routes):
    n_tok, width = tokens.shape
    hid = w_gate.shape[2]
    half = hid // 2
    n_lane = 4 * n_tok
    bf, f32 = jnp.bfloat16, jnp.float32
    vm = pl.BlockSpec(memory_space=pltpu.VMEM)
    hbm = pl.BlockSpec(memory_space=pl.ANY)
    out = jax.ShapeDtypeStruct((n_tok, width), f32)
    dma = pltpu.SemaphoreType.DMA
    keep = pltpu.VMEM((2, 2, 2 * n_lane, half), f32)

    def home(columns):
        return [
            pltpu.VMEM((3 * n_lane, columns), bf),
            pltpu.VMEM((n_lane, columns), f32),
            pltpu.VMEM((4, n_tok, columns), bf),
            pltpu.VMEM((2, n_lane, columns), bf),
            pltpu.VMEM((4, n_tok, columns), bf),
        ]

    image, gram = pl.pallas_call(
        block_kernel,
        out_shape=(out, out),
        in_specs=[vm] * 5 + [hbm] * 3,
        out_specs=(vm, vm),
        scratch_shapes=[
            pltpu.VMEM((2, width, 2 * hid), bf),
            pltpu.VMEM((2, hid, width), bf),
            pltpu.VMEM((3 * n_lane, 2 * width + 128), bf),
            keep, keep, keep,
            pltpu.VMEM((2, 2 * n_lane, hid), bf),
            *home(width),
            pltpu.VMEM((3 * n_lane, width), bf),
            pltpu.VMEM((2, 2 * n_lane, 2 * hid), bf),
            *home(width + 128),
            pltpu.VMEM((n_tok, 128), f32),
            pltpu.VMEM((n_tok, 128), f32),
            pltpu.VMEM((128, width), bf),
            dma((3, 2, 3)), dma((3, 2, 3)), dma((3, 2)),
            dma((3, 2, 4)), dma((3, 2, 4)),
            dma((3, 4)), dma((3, 4)), dma((3, 4)), dma((3, 4)),
            dma((2, 2, 4)), dma((2, 2, 4)), dma((2, 4)), dma((2, 4)),
        ],
        compiler_params=pltpu.CompilerParams(
            collective_id=0, has_side_effects=True, vmem_limit_bytes=60 * 2**20
        ),
        cost_estimate=pl.CostEstimate(
            flops=2 * 8 * 512 * width * hid, bytes_accessed=2**24, transcendentals=2**20
        ),
    )(tokens, tangent, norm_gain.reshape(1, width), router.T, routes.T, w_gate, w_up, w_down)
    return image, gram


def solution(mesh):
    in_specs = (
        P(("dp", "expert"), None),
        P(("dp", "expert"), None),
        P(),
        P(),
        P("expert", "dp", None),
        P("expert", "dp", None),
        P("expert", None, "dp"),
        P(("dp", "expert"), None),
    )
    out_specs = (P(("dp", "expert"), None), P(("dp", "expert"), None))
    body = on_device
    if mesh.shape["dp"] == 4 and mesh.shape["expert"] == 8:
        body = on_device_dense
    return jax.shard_map(
        body, mesh=mesh, in_specs=in_specs, out_specs=out_specs, check_vma=False
    )
```

time: 186 us -> 162 us (0.87)
  Pallas kernels: 179 us -> 158 us
  local copies, waits for them, and re-layouts: 6.71 us -> 3.34 us
    pallas_call x1, Pallas kernels: 179 us -> 158 us  [on_device_dense(): pl.pallas_call(block_kernel, out_shape=(out, out), in_specs=[vm] * 5 + [h...]
    unnamed x4 -> x2, local copies, waits for them, and re-layouts: 5.82 us -> 3.34 us
where the time goes in v1:
time: 162 us
  Pallas kernels  158 us (98%)
  local copies, waits for them, and re-layouts  3.34 us (2%)
    pallas_call x1, Pallas kernels, on_device_dense(): pl.pallas_call(block_kernel, out_shape=(out, out), in_specs=[vm] * 5 + [h...  158 us
    unnamed x2, local copies, waits for them, and re-layouts  3.34 us

profile of v1, /device:TPU:0, one launch (start us, length us, event | category | flops | bytes accessed | tf_op | source)
XLA Modules:
  0.0 161.9 jit_solution(6345911340607347606)
XLA Ops:
  0.6 158.0 %shard_map.95 = (f32[32,2048]{1,0:T(8,128)}, f32[32,2048]{1,0:T(8,128)}) custom-call(bf16[32,2048]{1,0:T(8,128)(2,1)} %tok_ref.1, bf16[32,2048]{1,0:T(8,128)(2,1)} %tan_ref.1, f32[1,2048]{1,0:T(1,128)} %bitcast.4, bf16[16,2048]{1,0:T(8,128)(2,1)} %bitcast.3, s32[8,32]{1,0:T(8,128)} %bitcast.5, bf16[2,512,768]{2,1,0:T(8,128)(2,1)} %wg_ref.1, ...), custom_call_target="tpu_custom_call" | custom-call | flops 12884901888 | bytes 16777216 | tf_op jit(solution)/shard_map/pallas_call | solution.py:492
  158.6 1.7 %copy.12 = f32[32,2048]{1,0:T(8,128)} copy(f32[32,2048]{1,0:T(8,128)} %get-tuple-element.4) | data formatting | bytes 524288
  160.3 1.7 %copy.13 = f32[32,2048]{1,0:T(8,128)} copy(f32[32,2048]{1,0:T(8,128)} %get-tuple-element.5) | data formatting | bytes 524288

commit v2 on v1

--- a/solution.py
+++ b/solution.py
@@ -163,6 +163,9 @@
     return jnp.dot(left, right, preferred_element_type=jnp.float32)
 
 
+batches = 2
+
+
 def block_kernel(
     tok_ref, tan_ref, gain_ref, router_ref, routes_ref, wg_ref, wu_ref, wd_ref,
     image_ref, gram_ref,
@@ -175,7 +178,8 @@
     n_tok, width = tok_ref.shape
     slab, hid = wg_ref.shape[1], wg_ref.shape[2]
     half = hid // 2
-    n_lane = 4 * n_tok
+    n_sub = n_tok // batches
+    n_lane = 4 * n_sub
     n_exp = router_ref.shape[0]
     dp, ex = lax.axis_index("dp"), lax.axis_index("expert")
     y, x = dp // 2, dp % 2
@@ -188,7 +192,10 @@
     at_x, at_own, at_y = 0, n_lane, 2 * n_lane
 
     def rows_of(base, dz):
-        return pl.ds(pl.multiple_of(base + (z + dz) % 4 * n_tok, n_tok), n_tok)
+        return pl.ds(pl.multiple_of(base + (z + dz) % 4 * n_sub, n_sub), n_sub)
+
+    def tokens_of(b):
+        return slice(b * n_sub, (b + 1) * n_sub)
 
     barrier = pltpu.get_barrier_semaphore()
     friends = z_peers + [x_peer, y_peer, mate]
@@ -276,8 +283,9 @@
     inv_cube = inv_rms * inv_rms * inv_rms
     normed_tan = (gain * (vfull * inv_rms - xfull * inv_cube * cross_term)).astype(bf)
     mine = rows_of(at_own, 0)
-    rows[mine, 0:width] = normed
-    rows[mine, width : 2 * width] = normed_tan
+    for b in range(batches):
+        rows[b, mine, 0:width] = normed[tokens_of(b)]
+        rows[b, mine, width : 2 * width] = normed_tan[tokens_of(b)]
     logits = nt_dot(normed, router_pad[...])
     logit_tan = nt_dot(normed_tan, router_pad[...])
     ids = lax.broadcasted_iota(jnp.int32, (128, n_tok), 0)
@@ -295,18 +303,18 @@
     gate_tan = gate_prob * (
         logit_tan - jnp.sum(gate_prob * logit_tan, axis=1, keepdims=True)
     )
-    rows[mine, 2 * width : 2 * width + 128] = (
-        gate_prob + pltpu.roll(gate_tan, 64, 1)
-    ).astype(bf)
+    table = (gate_prob + pltpu.roll(gate_tan, 64, 1)).astype(bf)
+    for b in range(batches):
+        rows[b, mine, 2 * width : 2 * width + 128] = table[tokens_of(b)]
     prob_keep[...] = gate_prob
     inv_keep[...] = jnp.broadcast_to(inv_rms, (n_tok, 128))
 
     def along_z(buf, base, sems, which):
-        block = buf.at[rows_of(base, 0)]
+        block = buf.at[:, rows_of(base, 0)]
         return [push(block, block, sems, (which, dz), z_peers[dz - 1]) for dz in (2, 1, 3)]
 
-    from_x = push(rows.at[mine], rows.at[rows_of(at_x, 0)], t_sems, (0, 0), x_peer)
-    from_y = push(rows.at[mine], rows.at[rows_of(at_y, 0)], t_sems, (2, 0), y_peer)
+    from_x = push(rows.at[:, mine], rows.at[:, rows_of(at_x, 0)], t_sems, (0, 0), x_peer)
+    from_y = push(rows.at[:, mine], rows.at[:, rows_of(at_y, 0)], t_sems, (2, 0), y_peer)
     token_copies = along_z(rows, at_own, t_sems, 1)
     pieces = [(0, 0), (1, 0), (0, 1), (1, 1), (2, 0), (2, 1)]
     for kind, l in pieces[1:]:
@@ -323,24 +331,27 @@
         copy.wait_recv()
 
     n_rows = 2 * n_lane
-    wide_lanes = lax.broadcasted_iota(jnp.int32, (n_rows, 128), 1)
+    all_rows = batches * n_rows
+    wide_lanes = lax.broadcasted_iota(jnp.int32, (all_rows, 128), 1)
 
     for l in range(2):
         need_weights(0, l)
         need_weights(1, l)
-        these = pl.ds(l * n_lane, n_rows)
+        these = slice(l * n_lane, l * n_lane + n_rows)
 
         @pl.loop(0, 2)
         def _(k):
             cols = pl.ds(pl.multiple_of(k * hid, hid), hid)
             expert = (z * 2 + k) * 2 + l
-            table = rows[these, 2 * width : 2 * width + 128].astype(f32)
+            table = rows[:, these, 2 * width : 2 * width + 128].reshape(all_rows, 128).astype(f32)
             gate = jnp.sum(jnp.where(wide_lanes == expert, table, 0.0), axis=1, keepdims=True)
             tan = jnp.sum(
                 jnp.where(wide_lanes == expert + 64, table, 0.0), axis=1, keepdims=True
             )
-            pre = nn_dot(rows[these, 0:width], wgu[l, :, cols])
-            dots = nn_dot(rows[these, width : 2 * width], wgu[l, :, cols])
+            pre = nn_dot(rows[:, these, 0:width].reshape(all_rows, width), wgu[l, :, cols])
+            dots = nn_dot(
+                rows[:, these, width : 2 * width].reshape(all_rows, width), wgu[l, :, cols]
+            )
             pre_gate, pre_up = pre[:, 0:half], pre[:, half:hid]
             gate_dot, up_dot = dots[:, 0:half], dots[:, half:hid]
             sig = jax.nn.sigmoid(pre_gate)
@@ -356,114 +367,149 @@
     for kind, l in pieces[4:]:
         last_weights(kind, l)
 
-    def send_side(parts, far, turn, s):
+    step = width // 4
+    turns = [
+        (part, own_part, mid, far, landed), (part2, own_part2, mid2, far2, landed2)
+    ]
+    x_copies, y_copies, z_copies, totals = {}, {}, {}, {}
+
+    def place(turn, b, l, cols, term):
+        parts, own = turns[turn][0:2]
+        if l == 0:
+            parts[b, at_x : at_x + n_lane, cols] = term[0:n_lane].astype(bf)
+            own[b, :, cols] = term[n_lane:n_rows]
+        else:
+            own[b, :, cols] = own[b, :, cols] + term[0:n_lane]
+            parts[b, at_y : at_y + n_lane, cols] = term[n_lane:n_rows].astype(bf)
+
+    def send_side(turn, b, s):
+        parts, far = turns[turn][0], turns[turn][3]
         peer, base = ((x_peer, at_x), (y_peer, at_y))[s]
-        return [
-            push(
-                parts.at[rows_of(base, dz)], far.at[s, rows_of(0, dz)],
-                s_sems, (turn, s, dz), peer,
+        copies = (x_copies, y_copies)[s]
+        for dz in (2, 1, 3, 0):
+            copies[turn, b, dz] = push(
+                parts.at[b, rows_of(base, dz)], far.at[b, s, rows_of(0, dz)],
+                s_sems, (turn, b, s, dz), peer,
             )
-            for dz in (2, 1, 3, 0)
-        ]
-
-    def send_home(compute, parts, own, mid, far, land, turn):
-        compute(0)
-        x_copies = send_side(parts, far, turn, 0)
-        compute(1)
-        y_copies = send_side(parts, far, turn, 1)
-        copies = {}
-        for i, dz in enumerate((2, 1, 3, 0)):
-            x_copies[i].wait_recv()
-            y_copies[i].wait_recv()
-            at = rows_of(0, dz)
-            total = own[at, :] + (far[0, at, :].astype(f32) + far[1, at, :].astype(f32))
-            if dz:
-                mid[dz] = total.astype(bf)
-                copies[dz] = push(
-                    mid.at[dz], land.at[z], z_sems, (turn, dz), z_peers[dz - 1]
-                )
+
+    def merge(turn, b, dz):
+        parts, own, mid, far, land = turns[turn]
+        x_copies[turn, b, dz].wait_recv()
+        y_copies[turn, b, dz].wait_recv()
+        at = rows_of(0, dz)
+        total = own[b, at, :] + (far[b, 0, at, :].astype(f32) + far[b, 1, at, :].astype(f32))
+        if dz:
+            mid[b, dz] = total.astype(bf)
+            z_copies[turn, b, dz] = push(
+                mid.at[b, dz], land.at[b, z], z_sems, (turn, b, dz), z_peers[dz - 1]
+            )
+        else:
+            own[b, at, :] = total
+
+    def total_of(turn, b):
+        own, land = turns[turn][1], turns[turn][4]
+        total = own[b, rows_of(0, 0), :]
         for dz in (1, 3, 2):
-            copies[dz].wait_recv()
-            total = total + land[(z + 4 - dz) % 4].astype(f32)
+            z_copies[turn, b, dz].wait_recv()
+            total = total + land[b, (z + 4 - dz) % 4].astype(f32)
         return total
 
-    step = width // 4
-
-    def place(parts, own, l, cols, term):
-        if l == 0:
-            parts[at_x : at_x + n_lane, cols] = term[0:n_lane].astype(bf)
-            own[:, cols] = term[n_lane:n_rows]
-        else:
-            own[:, cols] = own[:, cols] + term[0:n_lane]
-            parts[at_y : at_y + n_lane, cols] = term[n_lane:n_rows].astype(bf)
-
-    def down(l):
-        need_weights(2, l)
-
+    def down(b, l):
         @pl.loop(0, 4)
         def _(j):
             cols = pl.ds(pl.multiple_of(j * step, step), step)
-            place(part, own_part, l, cols, nn_dot(mix[l], wd[l, :, cols]))
-
-    image = send_home(down, part, own_part, mid, far, landed, 0)
-    image_ref[...] = image
-    image_rows[mine, :] = image.astype(bf)
-
-    def gather_image():
-        block = image_rows.at[mine]
-        to_z = {dz: push(block, block, a_sems, (0, dz), z_peers[dz - 1]) for dz in (2, 1, 3)}
-        sides = []
-
-        def to_sides(dz):
-            block = image_rows.at[rows_of(at_own, 4 - dz)]
-            for s, (peer, base) in enumerate(((x_peer, at_x), (y_peer, at_y))):
-                sides.append(
-                    push(block, image_rows.at[rows_of(base, 4 - dz)], a_sems, (1 + s, dz), peer)
-                )
-
-        to_sides(0)
-        for dz in (3, 1, 2):
-            to_z[dz].wait_recv()
-            to_sides(dz)
-        for copy in sides:
-            copy.wait_recv()
-
-    gather_image()
-
-    def backward(l):
-        these = pl.ds(l * n_lane, n_rows)
+            left = mix[l, b * n_rows : (b + 1) * n_rows, :]
+            place(0, b, l, cols, nn_dot(left, wd[l, :, cols]))
+
+        send_side(0, b, l)
+
+    to_z, sides = {}, {}
+
+    def image_to_sides(b, dz):
+        block = image_rows.at[b, rows_of(at_own, 4 - dz)]
+        for s, (peer, base) in enumerate(((x_peer, at_x), (y_peer, at_y))):
+            sides[b, s, dz] = push(
+                block, image_rows.at[b, rows_of(base, 4 - dz)], a_sems, (b, 1 + s, dz), peer
+            )
+
+    def image_of(b):
+        image = total_of(0, b)
+        image_ref[tokens_of(b), :] = image
+        image_rows[b, mine, :] = image.astype(bf)
+        block = image_rows.at[b, mine]
+        for dz in (2, 1, 3):
+            to_z[b, dz] = push(block, block, a_sems, (b, 0, dz), z_peers[dz - 1])
+        image_to_sides(b, 0)
+
+    def image_on(b, dz):
+        to_z[b, dz].wait_recv()
+        image_to_sides(b, dz)
+
+    def backward(b, l):
+        for dz in range(4):
+            sides[b, l, dz].wait_recv()
+        these = slice(l * n_lane, l * n_lane + n_rows)
+        kept = slice(b * n_rows, (b + 1) * n_rows)
         cots = jnp.zeros((n_rows, 128), f32)
         for k in range(2):
-            back = nt_dot(image_rows[these, :], wd[l, k * half : (k + 1) * half, :])
-            cot = jnp.sum(back * keep_h[l, k], axis=1, keepdims=True)
-            cots = cots + jnp.where(wide_lanes == (z * 2 + k) * 2 + l, cot, 0.0)
-            grads[l, :, k * hid : k * hid + half] = (back * keep_a[l, k]).astype(bf)
-            grads[l, :, k * hid + half : (k + 1) * hid] = (back * keep_s[l, k]).astype(bf)
-        place(part2, own_part2, l, slice(width, width + 128), cots)
+            back = nt_dot(image_rows[b, these, :], wd[l, k * half : (k + 1) * half, :])
+            cot = jnp.sum(back * keep_h[l, k, kept], axis=1, keepdims=True)
+            cots = cots + jnp.where(wide_lanes[0:n_rows] == (z * 2 + k) * 2 + l, cot, 0.0)
+            grads[l, :, k * hid : k * hid + half] = (back * keep_a[l, k, kept]).astype(bf)
+            grads[l, :, k * hid + half : (k + 1) * hid] = (back * keep_s[l, k, kept]).astype(bf)
+        place(1, b, l, slice(width, width + 128), cots)
 
         @pl.loop(0, 4)
         def _(j):
             cols = pl.ds(pl.multiple_of(j * step, step), step)
-            place(part2, own_part2, l, cols, nt_dot(grads[l], wgu[l, cols, :]))
-
-    total = send_home(backward, part2, own_part2, mid2, far2, landed2, 1)
-
-    expert_grad = total[:, 0:width]
-    cot = total[:, width : width + 128]
-    prob = prob_keep[...]
-    column_grad = prob * (cot - jnp.sum(prob * cot, axis=1, keepdims=True))
-    high = column_grad.astype(bf)
-    rest = column_grad - high.astype(f32)
-    middle = rest.astype(bf)
-    low = (rest - middle.astype(f32)).astype(bf)
-    router = router_pad[...]
-    router_grad = nn_dot(high, router) + (nn_dot(middle, router) + nn_dot(low, router))
-    xfull = tok_ref[...].astype(f32)
-    inv_rms = inv_keep[:, 0:1]
-    pulled = gain_ref[...] * (expert_grad + router_grad)
-    gram_ref[...] = inv_rms * pulled - xfull * (inv_rms * inv_rms * inv_rms) * jnp.mean(
-        pulled * xfull, axis=1, keepdims=True
-    )
+            place(1, b, l, cols, nt_dot(grads[l], wgu[l, cols, :]))
+
+        send_side(1, b, l)
+
+    def gram_of(b):
+        total = total_of(1, b)
+        these = tokens_of(b)
+        expert_grad = total[:, 0:width]
+        cot = total[:, width : width + 128]
+        prob = prob_keep[these, :]
+        column_grad = prob * (cot - jnp.sum(prob * cot, axis=1, keepdims=True))
+        high = column_grad.astype(bf)
+        rest = column_grad - high.astype(f32)
+        middle = rest.astype(bf)
+        low = (rest - middle.astype(f32)).astype(bf)
+        router = router_pad[...]
+        router_grad = nn_dot(high, router) + (nn_dot(middle, router) + nn_dot(low, router))
+        xfull = tok_ref[these, :].astype(f32)
+        inv_rms = inv_keep[these, 0:1]
+        pulled = gain_ref[...] * (expert_grad + router_grad)
+        gram_ref[these, :] = inv_rms * pulled - xfull * (inv_rms * inv_rms * inv_rms) * jnp.mean(
+            pulled * xfull, axis=1, keepdims=True
+        )
+
+    need_weights(2, 0)
+    down(0, 0)
+    need_weights(2, 1)
+    down(0, 1)
+    down(1, 0)
+    down(1, 1)
+    for b in range(batches):
+        for dz in (2, 1, 3, 0):
+            merge(0, b, dz)
+    for b in range(batches):
+        image_of(b)
+    for dz in (3, 1, 2):
+        image_on(0, dz)
+    backward(0, 0)
+    for dz in (3, 1, 2):
+        image_on(1, dz)
+    backward(0, 1)
+    backward(1, 0)
+    backward(1, 1)
+    for b in range(batches):
+        for dz in (2, 1, 3, 0):
+            merge(1, b, dz)
+    for b in range(batches):
+        gram_of(b)
     for copy in pending:
         copy.wait_send()
 
@@ -472,21 +518,23 @@
     n_tok, width = tokens.shape
     hid = w_gate.shape[2]
     half = hid // 2
-    n_lane = 4 * n_tok
+    n_sub = n_tok // batches
+    n_lane = 4 * n_sub
+    n_rows = 2 * n_lane
     bf, f32 = jnp.bfloat16, jnp.float32
     vm = pl.BlockSpec(memory_space=pltpu.VMEM)
     hbm = pl.BlockSpec(memory_space=pl.ANY)
     out = jax.ShapeDtypeStruct((n_tok, width), f32)
     dma = pltpu.SemaphoreType.DMA
-    keep = pltpu.VMEM((2, 2, 2 * n_lane, half), f32)
+    keep = pltpu.VMEM((2, 2, batches * n_rows, half), f32)
 
     def home(columns):
         return [
-            pltpu.VMEM((3 * n_lane, columns), bf),
-            pltpu.VMEM((n_lane, columns), f32),
-            pltpu.VMEM((4, n_tok, columns), bf),
-            pltpu.VMEM((2, n_lane, columns), bf),
-            pltpu.VMEM((4, n_tok, columns), bf),
+            pltpu.VMEM((batches, 3 * n_lane, columns), bf),
+            pltpu.VMEM((batches, n_lane, columns), f32),
+            pltpu.VMEM((batches, 4, n_sub, columns), bf),
+            pltpu.VMEM((batches, 2, n_lane, columns), bf),
+            pltpu.VMEM((batches, 4, n_sub, columns), bf),
         ]
 
     image, gram = pl.pallas_call(
@@ -497,20 +545,21 @@
         scratch_shapes=[
             pltpu.VMEM((2, width, 2 * hid), bf),
             pltpu.VMEM((2, hid, width), bf),
-            pltpu.VMEM((3 * n_lane, 2 * width + 128), bf),
+            pltpu.VMEM((batches, 3 * n_lane, 2 * width + 128), bf),
             keep, keep, keep,
-            pltpu.VMEM((2, 2 * n_lane, hid), bf),
+            pltpu.VMEM((2, batches * n_rows, hid), bf),
             *home(width),
-            pltpu.VMEM((3 * n_lane, width), bf),
-            pltpu.VMEM((2, 2 * n_lane, 2 * hid), bf),
+            pltpu.VMEM((batches, 3 * n_lane, width), bf),
+            pltpu.VMEM((2, n_rows, 2 * hid), bf),
             *home(width + 128),
             pltpu.VMEM((n_tok, 128), f32),
             pltpu.VMEM((n_tok, 128), f32),
             pltpu.VMEM((128, width), bf),
             dma((3, 2, 3)), dma((3, 2, 3)), dma((3, 2)),
             dma((3, 2, 4)), dma((3, 2, 4)),
-            dma((3, 4)), dma((3, 4)), dma((3, 4)), dma((3, 4)),
-            dma((2, 2, 4)), dma((2, 2, 4)), dma((2, 4)), dma((2, 4)),
+            dma((3, 4)), dma((3, 4)), dma((batches, 3, 4)), dma((batches, 3, 4)),
+            dma((2, batches, 2, 4)), dma((2, batches, 2, 4)),
+            dma((2, batches, 4)), dma((2, batches, 4)),
         ],
         compiler_params=pltpu.CompilerParams(
             collective_id=0, has_side_effects=True, vmem_limit_bytes=60 * 2**20

time: 162 us -> 162 us (level)
  Pallas kernels: 158 us -> 156 us
where the time goes in v2:
time: 162 us; the launch traced here: 160 us
  Pallas kernels  156 us (96%)
  local copies, waits for them, and re-layouts  3.34 us (2%)
    pallas_call x1, Pallas kernels, on_device_dense(): pl.pallas_call(block_kernel, out_shape=(out, out), in_specs=[vm] * 5 + [h...  156 us
    unnamed x2, local copies, waits for them, and re-layouts  3.34 us

profile of v2, /device:TPU:0, one launch (start us, length us, event | category | flops | bytes accessed | tf_op | source)
XLA Modules:
  0.0 160.5 jit_solution(10732999308490741958)
XLA Ops:
  0.6 156.5 %shard_map.95 = (f32[32,2048]{1,0:T(8,128)}, f32[32,2048]{1,0:T(8,128)}) custom-call(bf16[32,2048]{1,0:T(8,128)(2,1)} %tok_ref.1, bf16[32,2048]{1,0:T(8,128)(2,1)} %tan_ref.1, f32[1,2048]{1,0:T(1,128)} %bitcast.4, bf16[16,2048]{1,0:T(8,128)(2,1)} %bitcast.3, s32[8,32]{1,0:T(8,128)} %bitcast.5, bf16[2,512,768]{2,1,0:T(8,128)(2,1)} %wg_ref.1, ...), custom_call_target="tpu_custom_call" | custom-call | flops 12884901888 | bytes 16777216 | tf_op jit(solution)/shard_map/pallas_call | solution.py:540
  157.1 1.7 %copy.12 = f32[32,2048]{1,0:T(8,128)} copy(f32[32,2048]{1,0:T(8,128)} %get-tuple-element.4) | data formatting | bytes 524288
  158.8 1.7 %copy.13 = f32[32,2048]{1,0:T(8,128)} copy(f32[32,2048]{1,0:T(8,128)} %get-tuple-element.5) | data formatting | bytes 524288

commit v3 on v2

--- a/solution.py
+++ b/solution.py
@@ -169,7 +169,7 @@
 def block_kernel(
     tok_ref, tan_ref, gain_ref, router_ref, routes_ref, wg_ref, wu_ref, wd_ref,
     image_ref, gram_ref,
-    wgu, wd, rows, keep_a, keep_s, keep_h, mix, part, own_part, mid, far, landed,
+    wgu, wgu_t, wd, rows, keep_a, keep_s, keep_h, mix, part, own_part, mid, far, landed,
     image_rows, grads, part2, own_part2, mid2, far2, landed2, prob_keep, inv_keep, router_pad,
     w_send, w_recv, w_own, m_send, m_recv, t_send, t_recv, a_send, a_recv, s_send, s_recv,
     z_send, z_recv,
@@ -317,16 +317,29 @@
     from_y = push(rows.at[:, mine], rows.at[:, rows_of(at_y, 0)], t_sems, (2, 0), y_peer)
     token_copies = along_z(rows, at_own, t_sems, 1)
     pieces = [(0, 0), (1, 0), (0, 1), (1, 1), (2, 0), (2, 1)]
-    for kind, l in pieces[1:]:
-        start_weights(kind, l)
+    start_weights(1, 0)
     from_x.wait_recv()
     token_copies += along_z(rows, at_x, t_sems, 0)
     from_y.wait_recv()
     token_copies += along_z(rows, at_y, t_sems, 2)
-    for kind, l in pieces:
+
+    def turn_weights(l):
+        need_weights(0, l)
+        need_weights(1, l)
+
+        @pl.loop(0, 4)
+        def _(j):
+            at = pl.ds(pl.multiple_of(j * slab, slab), slab)
+            wgu_t[l, :, at] = wgu[l, at, :].T
+
+    for i, (kind, l) in enumerate(pieces):
         relay_weights(kind, l)
-    for kind, l in pieces[:4]:
-        last_weights(kind, l)
+        if i + 2 < len(pieces):
+            start_weights(*pieces[i + 2])
+        if 1 <= i <= 4:
+            last_weights(*pieces[i - 1])
+        if i in (2, 4):
+            turn_weights(i // 2 - 1)
     for copy in token_copies:
         copy.wait_recv()
 
@@ -335,8 +348,6 @@
     wide_lanes = lax.broadcasted_iota(jnp.int32, (all_rows, 128), 1)
 
     for l in range(2):
-        need_weights(0, l)
-        need_weights(1, l)
         these = slice(l * n_lane, l * n_lane + n_rows)
 
         @pl.loop(0, 2)
@@ -364,10 +375,8 @@
             keep_h[l, k] = hidden
             mix[l, :, pl.ds(pl.multiple_of(k * half, half), half)] = mixed.astype(bf)
 
-    for kind, l in pieces[4:]:
-        last_weights(kind, l)
-
-    step = width // 4
+        last_weights(2, l)
+
     turns = [
         (part, own_part, mid, far, landed), (part2, own_part2, mid2, far2, landed2)
     ]
@@ -415,12 +424,8 @@
         return total
 
     def down(b, l):
-        @pl.loop(0, 4)
-        def _(j):
-            cols = pl.ds(pl.multiple_of(j * step, step), step)
-            left = mix[l, b * n_rows : (b + 1) * n_rows, :]
-            place(0, b, l, cols, nn_dot(left, wd[l, :, cols]))
-
+        left = mix[l, b * n_rows : (b + 1) * n_rows, :]
+        place(0, b, l, slice(0, width), nn_dot(left, wd[l]))
         send_side(0, b, l)
 
     to_z, sides = {}, {}
@@ -451,19 +456,15 @@
         these = slice(l * n_lane, l * n_lane + n_rows)
         kept = slice(b * n_rows, (b + 1) * n_rows)
         cots = jnp.zeros((n_rows, 128), f32)
+        back_both = nt_dot(image_rows[b, these, :], wd[l])
         for k in range(2):
-            back = nt_dot(image_rows[b, these, :], wd[l, k * half : (k + 1) * half, :])
+            back = back_both[:, k * half : (k + 1) * half]
             cot = jnp.sum(back * keep_h[l, k, kept], axis=1, keepdims=True)
             cots = cots + jnp.where(wide_lanes[0:n_rows] == (z * 2 + k) * 2 + l, cot, 0.0)
             grads[l, :, k * hid : k * hid + half] = (back * keep_a[l, k, kept]).astype(bf)
             grads[l, :, k * hid + half : (k + 1) * hid] = (back * keep_s[l, k, kept]).astype(bf)
         place(1, b, l, slice(width, width + 128), cots)
-
-        @pl.loop(0, 4)
-        def _(j):
-            cols = pl.ds(pl.multiple_of(j * step, step), step)
-            place(1, b, l, cols, nt_dot(grads[l], wgu[l, cols, :]))
-
+        place(1, b, l, slice(0, width), nn_dot(grads[l], wgu_t[l]))
         send_side(1, b, l)
 
     def gram_of(b):
@@ -487,29 +488,41 @@
         )
 
     need_weights(2, 0)
-    down(0, 0)
+    down(0,0)
     need_weights(2, 1)
-    down(0, 1)
-    down(1, 0)
-    down(1, 1)
-    for b in range(batches):
-        for dz in (2, 1, 3, 0):
-            merge(0, b, dz)
-    for b in range(batches):
-        image_of(b)
-    for dz in (3, 1, 2):
-        image_on(0, dz)
-    backward(0, 0)
-    for dz in (3, 1, 2):
-        image_on(1, dz)
-    backward(0, 1)
-    backward(1, 0)
-    backward(1, 1)
-    for b in range(batches):
-        for dz in (2, 1, 3, 0):
-            merge(1, b, dz)
-    for b in range(batches):
-        gram_of(b)
+    down(0,1)
+    down(1,0)
+    down(1,1)
+    merge(0,0,2)
+    merge(0,0,1)
+    merge(0,0,3)
+    merge(0,0,0)
+    merge(0,1,2)
+    merge(0,1,1)
+    image_of(0)
+    merge(0,1,3)
+    merge(0,1,0)
+    image_on(0,3)
+    image_on(0,1)
+    image_of(1)
+    image_on(0,2)
+    image_on(1,3)
+    image_on(1,1)
+    image_on(1,2)
+    backward(0,0)
+    backward(0,1)
+    backward(1,0)
+    backward(1,1)
+    merge(1,0,2)
+    merge(1,0,1)
+    merge(1,0,3)
+    merge(1,0,0)
+    merge(1,1,2)
+    merge(1,1,1)
+    merge(1,1,3)
+    merge(1,1,0)
+    gram_of(0)
+    gram_of(1)
     for copy in pending:
         copy.wait_send()
 
@@ -544,6 +557,7 @@
         out_specs=(vm, vm),
         scratch_shapes=[
             pltpu.VMEM((2, width, 2 * hid), bf),
+            pltpu.VMEM((2, 2 * hid, width), bf),
             pltpu.VMEM((2, hid, width), bf),
             pltpu.VMEM((batches, 3 * n_lane, 2 * width + 128), bf),
             keep, keep, keep,

time: 162 us -> 155 us (0.957)
  Pallas kernels: 156 us -> 151 us
    pallas_call x1, Pallas kernels: 156 us -> 151 us  [on_device_dense(): pl.pallas_call(block_kernel, out_shape=(out, out), in_specs=[vm] * 5 + [h...]
where the time goes in v3:
time: 155 us
  Pallas kernels  151 us (97%)
  local copies, waits for them, and re-layouts  3.34 us (2%)
    pallas_call x1, Pallas kernels, on_device_dense(): pl.pallas_call(block_kernel, out_shape=(out, out), in_specs=[vm] * 5 + [h...  151 us
    unnamed x2, local copies, waits for them, and re-layouts  3.34 us

profile of v3, /device:TPU:0, one launch (start us, length us, event | category | flops | bytes accessed | tf_op | source)
XLA Modules:
  0.0 154.5 jit_solution(904380406173071175)
XLA Ops:
  0.6 150.5 %shard_map.95 = (f32[32,2048]{1,0:T(8,128)}, f32[32,2048]{1,0:T(8,128)}) custom-call(bf16[32,2048]{1,0:T(8,128)(2,1)} %tok_ref.1, bf16[32,2048]{1,0:T(8,128)(2,1)} %tan_ref.1, f32[1,2048]{1,0:T(1,128)} %bitcast.4, bf16[16,2048]{1,0:T(8,128)(2,1)} %bitcast.3, s32[8,32]{1,0:T(8,128)} %bitcast.5, bf16[2,512,768]{2,1,0:T(8,128)(2,1)} %wg_ref.1, ...), custom_call_target="tpu_custom_call" | custom-call | flops 12884901888 | bytes 16777216 | tf_op jit(solution)/shard_map/pallas_call | solution.py:553
  151.2 1.7 %copy.12 = f32[32,2048]{1,0:T(8,128)} copy(f32[32,2048]{1,0:T(8,128)} %get-tuple-element.4) | data formatting | bytes 524288
  152.8 1.7 %copy.13 = f32[32,2048]{1,0:T(8,128)} copy(f32[32,2048]{1,0:T(8,128)} %get-tuple-element.5) | data formatting | bytes 524288

commit v4 on v3

--- a/solution.py
+++ b/solution.py
@@ -1,3 +1,5 @@
+import functools
+
 import jax
 import jax.numpy as jnp
 from jax import lax
@@ -168,7 +170,7 @@
 
 def block_kernel(
     tok_ref, tan_ref, gain_ref, router_ref, routes_ref, wg_ref, wu_ref, wd_ref,
-    image_ref, gram_ref,
+    both_ref,
     wgu, wgu_t, wd, rows, keep_a, keep_s, keep_h, mix, part, own_part, mid, far, landed,
     image_rows, grads, part2, own_part2, mid2, far2, landed2, prob_keep, inv_keep, router_pad,
     w_send, w_recv, w_own, m_send, m_recv, t_send, t_recv, a_send, a_recv, s_send, s_recv,
@@ -198,20 +200,33 @@
         return slice(b * n_sub, (b + 1) * n_sub)
 
     barrier = pltpu.get_barrier_semaphore()
-    friends = z_peers + [x_peer, y_peer, mate]
-    for friend in friends:
+    friends = [
+        (x_peer, None), (y_peer, None), (mate, None), (z_peers[0], z < 3), (z_peers[2], z > 0)
+    ]
+
+    def greet(friend):
         pl.semaphore_signal(barrier, inc=1, device_id=friend, device_id_type=MESH)
-    pl.semaphore_wait(barrier, len(friends))
+
+    for friend, cond in friends:
+        if cond is None:
+            greet(friend)
+        else:
+            pl.when(cond)(functools.partial(greet, friend))
+    inner = jnp.where(z > 0, 1, 0) * jnp.where(z < 3, 1, 0)
+    pl.semaphore_wait(barrier, 4 + inner)
 
     pending = []
 
-    def push(src, dst, sems, where, device):
+    def push(src, dst, sems, where, device, cond=None):
         copy = pltpu.make_async_remote_copy(
             src_ref=src, dst_ref=dst, send_sem=sems[0].at[where], recv_sem=sems[1].at[where],
             device_id=device, device_id_type=MESH,
         )
-        copy.start()
-        pending.append(copy)
+        if cond is None:
+            copy.start()
+        else:
+            pl.when(cond)(copy.start)
+        pending.append((copy, cond))
         return copy
 
     def slab_of(index):
@@ -233,33 +248,40 @@
     w_sems, m_sems, t_sems = (w_send, w_recv), (m_send, m_recv), (t_send, t_recv)
     a_sems, s_sems, z_sems = (a_send, a_recv), (s_send, s_recv), (z_send, z_recv)
 
-    def start_weights(kind, l):
-        mine = weight_at(kind, l, dp)
-        for_x, for_y = (1 - x, x) if l == 0 else (y, 1 - y)
-        for_me = x if l == 0 else y
-        direct[kind, l] = [
-            push(weight_src(kind, l, for_x), mine, w_sems, (kind, l, 0), x_peer),
-            push(weight_src(kind, l, for_y), mine, w_sems, (kind, l, 1), y_peer),
-        ]
-        local[kind, l] = pltpu.make_async_copy(
-            weight_src(kind, l, for_me), mine, w_own.at[kind, l]
-        )
-        local[kind, l].start()
-        shared[kind, l] = [
-            push(weight_src(kind, l, for_me), mine, m_sems, (kind, l, 0), mate)
-        ]
+    def start_weights(kind):
+        for p, l in ((0, 0), (1, 1), (0, 1), (1, 0)):
+            for_x, for_y = (1 - x, x) if l == 0 else (y, 1 - y)
+            direct[kind, l, p] = push(
+                weight_src(kind, l, (for_x, for_y)[p]), weight_at(kind, l, dp),
+                w_sems, (kind, l, p), (x_peer, y_peer)[p],
+            )
+        for l in range(2):
+            for_me = (x, y)[l]
+            mine = weight_at(kind, l, dp)
+            local[kind, l] = pltpu.make_async_copy(
+                weight_src(kind, l, for_me), mine, w_own.at[kind, l]
+            )
+            local[kind, l].start()
+            shared[kind, l] = [
+                push(weight_src(kind, l, for_me), mine, m_sems, (kind, l, 0), mate)
+            ]
 
     def share_weights(kind, l, slot, index):
         block = weight_at(kind, l, index)
         shared[kind, l].append(push(block, block, m_sems, (kind, l, slot), mate))
 
-    def relay_weights(kind, l):
-        block = weight_at(kind, l, (x_index, y_index)[l])
-        direct[kind, l][l].wait_recv()
-        relayed[kind, l] = push(block, block, w_sems, (kind, l, 2), (y_peer, x_peer)[l])
-        share_weights(kind, l, 1, (x_index, y_index)[l])
-        direct[kind, l][1 - l].wait_recv()
-        share_weights(kind, l, 2, (x_index, y_index)[1 - l])
+    def relay_weights(kind):
+        for l in range(2):
+            index = (x_index, y_index)[l]
+            block = weight_at(kind, l, index)
+            direct[kind, l, l].wait_recv()
+            relayed[kind, l] = push(block, block, w_sems, (kind, l, 2), (y_peer, x_peer)[l])
+            share_weights(kind, l, 1, index)
+
+    def side_weights(kind):
+        for l in range(2):
+            direct[kind, l, 1 - l].wait_recv()
+            share_weights(kind, l, 2, (x_index, y_index)[1 - l])
 
     def last_weights(kind, l):
         relayed[kind, l].wait_recv()
@@ -270,7 +292,7 @@
         for copy in shared[kind, l]:
             copy.wait_recv()
 
-    start_weights(0, 0)
+    start_weights(0)
 
     router_pad[...] = jnp.zeros(router_pad.shape, bf)
     router_pad[0:n_exp, :] = router_ref[...]
@@ -309,19 +331,45 @@
     prob_keep[...] = gate_prob
     inv_keep[...] = jnp.broadcast_to(inv_rms, (n_tok, 128))
 
-    def along_z(buf, base, sems, which):
-        block = buf.at[:, rows_of(base, 0)]
-        return [push(block, block, sems, (which, dz), z_peers[dz - 1]) for dz in (2, 1, 3)]
-
-    from_x = push(rows.at[:, mine], rows.at[:, rows_of(at_x, 0)], t_sems, (0, 0), x_peer)
-    from_y = push(rows.at[:, mine], rows.at[:, rows_of(at_y, 0)], t_sems, (2, 0), y_peer)
-    token_copies = along_z(rows, at_own, t_sems, 1)
-    pieces = [(0, 0), (1, 0), (0, 1), (1, 1), (2, 0), (2, 1)]
-    start_weights(1, 0)
+    ups, downs = {}, {}
+    bases = (at_x, at_own, at_y)
+
+    def has_up(j):
+        return jnp.logical_and(z < 3, z >= j)
+
+    def has_down(j):
+        return jnp.logical_and(z > 0, z + j <= 3)
+
+    def chain(which, j):
+        if j:
+            pl.when(z >= j)(ups[which, j - 1].wait_recv)
+            pl.when(z + j <= 3)(downs[which, j - 1].wait_recv)
+        if j < 3:
+            above = rows.at[:, rows_of(bases[which], 4 - j)]
+            below = rows.at[:, rows_of(bases[which], j)]
+            ups[which, j] = push(above, above, t_sems, (which, 0, j), z_peers[0], has_up(j))
+            downs[which, j] = push(below, below, t_sems, (which, 1, j), z_peers[2], has_down(j))
+
+    from_x = push(rows.at[:, mine], rows.at[:, rows_of(at_x, 0)], t_sems, (0, 2, 0), x_peer)
+    from_y = push(rows.at[:, mine], rows.at[:, rows_of(at_y, 0)], t_sems, (2, 2, 0), y_peer)
+    chain(1, 0)
+    start_weights(1)
     from_x.wait_recv()
-    token_copies += along_z(rows, at_x, t_sems, 0)
+    chain(0, 0)
     from_y.wait_recv()
-    token_copies += along_z(rows, at_y, t_sems, 2)
+    chain(2, 0)
+    relay_weights(0)
+    for which in (1, 0, 2):
+        chain(which, 1)
+    side_weights(0)
+    relay_weights(1)
+    start_weights(2)
+    for which in (1, 0, 2):
+        chain(which, 2)
+    side_weights(1)
+    for kind in range(2):
+        for l in range(2):
+            last_weights(kind, l)
 
     def turn_weights(l):
         need_weights(0, l)
@@ -332,16 +380,12 @@
             at = pl.ds(pl.multiple_of(j * slab, slab), slab)
             wgu_t[l, :, at] = wgu[l, at, :].T
 
-    for i, (kind, l) in enumerate(pieces):
-        relay_weights(kind, l)
-        if i + 2 < len(pieces):
-            start_weights(*pieces[i + 2])
-        if 1 <= i <= 4:
-            last_weights(*pieces[i - 1])
-        if i in (2, 4):
-            turn_weights(i // 2 - 1)
-    for copy in token_copies:
-        copy.wait_recv()
+    turn_weights(0)
+    turn_weights(1)
+    relay_weights(2)
+    side_weights(2)
+    for which in (1, 0, 2):
+        chain(which, 3)
 
     n_rows = 2 * n_lane
     all_rows = batches * n_rows
@@ -375,8 +419,6 @@
             keep_h[l, k] = hidden
             mix[l, :, pl.ds(pl.multiple_of(k * half, half), half)] = mixed.astype(bf)
 
-        last_weights(2, l)
-
     turns = [
         (part, own_part, mid, far, landed), (part2, own_part2, mid2, far2, landed2)
     ]
@@ -439,7 +481,7 @@
 
     def image_of(b):
         image = total_of(0, b)
-        image_ref[tokens_of(b), :] = image
+        both_ref[tokens_of(b), 0:width] = image
         image_rows[b, mine, :] = image.astype(bf)
         block = image_rows.at[b, mine]
         for dz in (2, 1, 3):
@@ -483,10 +525,12 @@
         xfull = tok_ref[these, :].astype(f32)
         inv_rms = inv_keep[these, 0:1]
         pulled = gain_ref[...] * (expert_grad + router_grad)
-        gram_ref[these, :] = inv_rms * pulled - xfull * (inv_rms * inv_rms * inv_rms) * jnp.mean(
+        both_ref[these, width : 2 * width] = inv_rms * pulled - xfull * (inv_rms * inv_rms * inv_rms) * jnp.mean(
             pulled * xfull, axis=1, keepdims=True
         )
 
+    last_weights(2, 0)
+    last_weights(2, 1)
     need_weights(2, 0)
     down(0,0)
     need_weights(2, 1)
@@ -523,8 +567,11 @@
     merge(1,1,0)
     gram_of(0)
     gram_of(1)
-    for copy in pending:
-        copy.wait_send()
+    for copy, cond in pending:
+        if cond is None:
+            copy.wait_send()
+        else:
+            pl.when(cond)(copy.wait_send)
 
 
 def on_device_dense(tokens, tangent, norm_gain, router, w_gate, w_up, w_down, routes):
@@ -537,7 +584,7 @@
     bf, f32 = jnp.bfloat16, jnp.float32
     vm = pl.BlockSpec(memory_space=pltpu.VMEM)
     hbm = pl.BlockSpec(memory_space=pl.ANY)
-    out = jax.ShapeDtypeStruct((n_tok, width), f32)
+    out = jax.ShapeDtypeStruct((n_tok, 2 * width), f32)
     dma = pltpu.SemaphoreType.DMA
     keep = pltpu.VMEM((2, 2, batches * n_rows, half), f32)
 
@@ -550,11 +597,11 @@
             pltpu.VMEM((batches, 4, n_sub, columns), bf),
         ]
 
-    image, gram = pl.pallas_call(
+    both = pl.pallas_call(
         block_kernel,
-        out_shape=(out, out),
+        out_shape=out,
         in_specs=[vm] * 5 + [hbm] * 3,
-        out_specs=(vm, vm),
+        out_specs=vm,
         scratch_shapes=[
             pltpu.VMEM((2, width, 2 * hid), bf),
             pltpu.VMEM((2, 2 * hid, width), bf),
@@ -571,7 +618,7 @@
             pltpu.VMEM((128, width), bf),
             dma((3, 2, 3)), dma((3, 2, 3)), dma((3, 2)),
             dma((3, 2, 4)), dma((3, 2, 4)),
-            dma((3, 4)), dma((3, 4)), dma((batches, 3, 4)), dma((batches, 3, 4)),
+            dma((3, 3, 3)), dma((3, 3, 3)), dma((batches, 3, 4)), dma((batches, 3, 4)),
             dma((2, batches, 2, 4)), dma((2, batches, 2, 4)),
             dma((2, batches, 4)), dma((2, batches, 4)),
         ],
@@ -582,7 +629,7 @@
             flops=2 * 8 * 512 * width * hid, bytes_accessed=2**24, transcendentals=2**20
         ),
     )(tokens, tangent, norm_gain.reshape(1, width), router.T, routes.T, w_gate, w_up, w_down)
-    return image, gram
+    return both[:, 0:width], both[:, width : 2 * width]
 
 
 def solution(mesh):

time: 155 us -> 150 us (0.968)
  Pallas kernels: 151 us -> 148 us
    unnamed x2 -> x0, local copies, waits for them, and re-layouts: 3.34 us -> none
    pallas_call x1, Pallas kernels: 151 us -> 148 us  [on_device_dense(): pl.pallas_call(block_kernel, out_shape=out, in_specs=[vm] * 5 + [hbm] * 3...]
    slice x0 -> x1, local copies, waits for them, and re-layouts: none -> 1.86 us  [on_device_dense(): return (both[:, 0:width], both[:, width:2 * width])]
where the time goes in v4:
time: 150 us
  Pallas kernels  148 us (99%)
  local copies, waits for them, and re-layouts  1.86 us (1%)
    pallas_call x1, Pallas kernels, on_device_dense(): pl.pallas_call(block_kernel, out_shape=out, in_specs=[vm] * 5 + [hbm] * 3...  148 us

profile of v4, /device:TPU:0, one launch (start us, length us, event | category | flops | bytes accessed | tf_op | source)
XLA Modules:
  0.0 150.2 jit_solution(17016785584655242666)
XLA Ops:
  0.6 147.7 %shard_map.95 = f32[32,4096]{1,0:T(8,128)} custom-call(bf16[32,2048]{1,0:T(8,128)(2,1)} %tok_ref.1, bf16[32,2048]{1,0:T(8,128)(2,1)} %tan_ref.1, f32[1,2048]{1,0:T(1,128)} %bitcast.4, bf16[16,2048]{1,0:T(8,128)(2,1)} %bitcast.3, s32[8,32]{1,0:T(8,128)} %bitcast.5, bf16[2,512,768]{2,1,0:T(8,128)(2,1)} %wg_ref.1, bf16[2,512,768]{2,1,0:T(8,128)(2,1)} %wu_ref.1, ...), custom_call_target="tpu_custom_call" | custom-call | flops 12884901888 | bytes 16777216 | tf_op jit(solution)/shard_map/pallas_call | solution.py:600
  148.3 1.9 %fusion = (f32[32,2048]{1,0:T(8,128)}, f32[32,2048]{1,0:T(8,128)}) fusion(f32[32,4096]{1,0:T(8,128)} %shard_map.95), kind=kLoop, calls=%fused_computation | loop fusion | bytes 1048576 | tf_op jit(solution)/shard_map/slice | solution.py:632

commit v5 on v4

--- a/solution.py
+++ b/solution.py
@@ -169,12 +169,13 @@
 
 
 def block_kernel(
-    tok_ref, tan_ref, gain_ref, router_ref, routes_ref, wg_ref, wu_ref, wd_ref,
-    both_ref,
+    tok_hbm, tan_hbm, gain_hbm, router_hbm, routes_hbm, wg_ref, wu_ref, wd_ref,
+    both_hbm,
+    tok_ref, tan_ref, gain_ref, router_ref, routes_ref, both_ref,
     wgu, wgu_t, wd, rows, keep_a, keep_s, keep_h, mix, part, own_part, mid, far, landed,
     image_rows, grads, part2, own_part2, mid2, far2, landed2, prob_keep, inv_keep, router_pad,
     w_send, w_recv, w_own, m_send, m_recv, t_send, t_recv, a_send, a_recv, s_send, s_recv,
-    z_send, z_recv,
+    z_send, z_recv, l_send, l_recv, i_sems, o_sems,
 ):
     f32, bf = jnp.float32, jnp.bfloat16
     n_tok, width = tok_ref.shape
@@ -199,6 +200,16 @@
     def tokens_of(b):
         return slice(b * n_sub, (b + 1) * n_sub)
 
+    loads = [
+        pltpu.make_async_copy(src, dst, i_sems.at[i])
+        for i, (src, dst) in enumerate((
+            (tok_hbm, tok_ref), (tan_hbm, tan_ref), (gain_hbm, gain_ref),
+            (router_hbm, router_ref), (routes_hbm, routes_ref),
+        ))
+    ]
+    for load in loads:
+        load.start()
+
     barrier = pltpu.get_barrier_semaphore()
     friends = [
         (x_peer, None), (y_peer, None), (mate, None), (z_peers[0], z < 3), (z_peers[2], z > 0)
@@ -247,6 +258,7 @@
     direct, relayed, shared, local = {}, {}, {}, {}
     w_sems, m_sems, t_sems = (w_send, w_recv), (m_send, m_recv), (t_send, t_recv)
     a_sems, s_sems, z_sems = (a_send, a_recv), (s_send, s_recv), (z_send, z_recv)
+    l_sems = (l_send, l_recv)
 
     def start_weights(kind):
         for p, l in ((0, 0), (1, 1), (0, 1), (1, 0)):
@@ -294,6 +306,8 @@
 
     start_weights(0)
 
+    for load in loads:
+        load.wait()
     router_pad[...] = jnp.zeros(router_pad.shape, bf)
     router_pad[0:n_exp, :] = router_ref[...]
     xfull = tok_ref[...].astype(f32)
@@ -470,27 +484,43 @@
         place(0, b, l, slice(0, width), nn_dot(left, wd[l]))
         send_side(0, b, l)
 
-    to_z, sides = {}, {}
-
-    def image_to_sides(b, dz):
+    links, sides, stores = {}, {}, []
+
+    def store(b, part):
+        piece = (tokens_of(b), pl.ds(part * width, width))
+        stores.append(
+            pltpu.make_async_copy(both_ref.at[piece], both_hbm.at[piece], o_sems.at[b, part])
+        )
+        stores[-1].start()
+
+    def image_to_sides(b, dz, cond=None):
         block = image_rows.at[b, rows_of(at_own, 4 - dz)]
         for s, (peer, base) in enumerate(((x_peer, at_x), (y_peer, at_y))):
             sides[b, s, dz] = push(
-                block, image_rows.at[b, rows_of(base, 4 - dz)], a_sems, (b, 1 + s, dz), peer
+                block, image_rows.at[b, rows_of(base, 4 - dz)], a_sems, (b, s, dz), peer, cond
             )
+
+    def image_link(b, way, j):
+        block = image_rows.at[b, rows_of(at_own, (4 - j, j)[way])]
+        links[b, way, j] = push(
+            block, block, l_sems, (b, way, j), z_peers[(0, 2)[way]], (has_up, has_down)[way](j)
+        )
 
     def image_of(b):
         image = total_of(0, b)
         both_ref[tokens_of(b), 0:width] = image
         image_rows[b, mine, :] = image.astype(bf)
-        block = image_rows.at[b, mine]
-        for dz in (2, 1, 3):
-            to_z[b, dz] = push(block, block, a_sems, (b, 0, dz), z_peers[dz - 1])
+        image_link(b, 0, 0)
+        image_link(b, 1, 0)
         image_to_sides(b, 0)
-
-    def image_on(b, dz):
-        to_z[b, dz].wait_recv()
-        image_to_sides(b, dz)
+        store(b, 0)
+
+    def image_on(b, j):
+        for way, here, dz in ((0, z > j, 1 + j), (1, z < 3 - j, 3 - j)):
+            pl.when(here)(links[b, way, j].wait_recv)
+            if j < 2:
+                image_link(b, way, j + 1)
+            image_to_sides(b, dz, here)
 
     def backward(b, l):
         for dz in range(4):
@@ -528,45 +558,48 @@
         both_ref[these, width : 2 * width] = inv_rms * pulled - xfull * (inv_rms * inv_rms * inv_rms) * jnp.mean(
             pulled * xfull, axis=1, keepdims=True
         )
+        store(b, 1)
 
     last_weights(2, 0)
     last_weights(2, 1)
     need_weights(2, 0)
-    down(0,0)
+    down(0, 0)
     need_weights(2, 1)
-    down(0,1)
-    down(1,0)
-    down(1,1)
-    merge(0,0,2)
-    merge(0,0,1)
-    merge(0,0,3)
-    merge(0,0,0)
-    merge(0,1,2)
-    merge(0,1,1)
+    down(0, 1)
+    down(1, 0)
+    down(1, 1)
+    merge(0, 0, 2)
+    merge(0, 0, 1)
+    merge(0, 0, 3)
+    merge(0, 0, 0)
+    merge(0, 1, 2)
+    merge(0, 1, 1)
     image_of(0)
-    merge(0,1,3)
-    merge(0,1,0)
-    image_on(0,3)
-    image_on(0,1)
+    merge(0, 1, 3)
+    merge(0, 1, 0)
+    image_on(0, 0)
+    image_on(0, 1)
     image_of(1)
-    image_on(0,2)
-    image_on(1,3)
-    image_on(1,1)
-    image_on(1,2)
-    backward(0,0)
-    backward(0,1)
-    backward(1,0)
-    backward(1,1)
-    merge(1,0,2)
-    merge(1,0,1)
-    merge(1,0,3)
-    merge(1,0,0)
-    merge(1,1,2)
-    merge(1,1,1)
-    merge(1,1,3)
-    merge(1,1,0)
+    image_on(0, 2)
+    image_on(1, 0)
+    image_on(1, 1)
+    image_on(1, 2)
+    backward(0, 0)
+    backward(0, 1)
+    backward(1, 0)
+    backward(1, 1)
+    merge(1, 0, 2)
+    merge(1, 0, 1)
+    merge(1, 0, 3)
+    merge(1, 0, 0)
+    merge(1, 1, 2)
+    merge(1, 1, 1)
+    merge(1, 1, 3)
+    merge(1, 1, 0)
     gram_of(0)
     gram_of(1)
+    for copy in stores:
+        copy.wait()
     for copy, cond in pending:
         if cond is None:
             copy.wait_send()
@@ -582,7 +615,6 @@
     n_lane = 4 * n_sub
     n_rows = 2 * n_lane
     bf, f32 = jnp.bfloat16, jnp.float32
-    vm = pl.BlockSpec(memory_space=pltpu.VMEM)
     hbm = pl.BlockSpec(memory_space=pl.ANY)
     out = jax.ShapeDtypeStruct((n_tok, 2 * width), f32)
     dma = pltpu.SemaphoreType.DMA
@@ -600,9 +632,15 @@
     both = pl.pallas_call(
         block_kernel,
         out_shape=out,
-        in_specs=[vm] * 5 + [hbm] * 3,
-        out_specs=vm,
+        in_specs=[hbm] * 8,
+        out_specs=hbm,
         scratch_shapes=[
+            pltpu.VMEM((n_tok, width), bf),
+            pltpu.VMEM((n_tok, width), bf),
+            pltpu.VMEM((1, width), f32),
+            pltpu.VMEM((router.shape[1], width), bf),
+            pltpu.VMEM((routes.shape[1], n_tok), routes.dtype),
+            pltpu.VMEM((n_tok, 2 * width), f32),
             pltpu.VMEM((2, width, 2 * hid), bf),
             pltpu.VMEM((2, 2 * hid, width), bf),
             pltpu.VMEM((2, hid, width), bf),
@@ -618,9 +656,10 @@
             pltpu.VMEM((128, width), bf),
             dma((3, 2, 3)), dma((3, 2, 3)), dma((3, 2)),
             dma((3, 2, 4)), dma((3, 2, 4)),
-            dma((3, 3, 3)), dma((3, 3, 3)), dma((batches, 3, 4)), dma((batches, 3, 4)),
+            dma((3, 3, 3)), dma((3, 3, 3)), dma((batches, 2, 4)), dma((batches, 2, 4)),
             dma((2, batches, 2, 4)), dma((2, batches, 2, 4)),
             dma((2, batches, 4)), dma((2, batches, 4)),
+            dma((batches, 2, 3)), dma((batches, 2, 3)), dma((5,)), dma((batches, 2)),
         ],
         compiler_params=pltpu.CompilerParams(
             collective_id=0, has_side_effects=True, vmem_limit_bytes=60 * 2**20

time: 150 us -> 147 us (0.980)
  Pallas kernels: 148 us -> 144 us
    pallas_call x1, Pallas kernels: 148 us -> 144 us  [on_device_dense(): pl.pallas_call(block_kernel, out_shape=out, in_specs=[hbm] * 8, out_specs...]
where the time goes in v5:
time: 147 us; the launch traced here: 146 us
  Pallas kernels  144 us (98%)
  local copies, waits for them, and re-layouts  1.86 us (1%)
    pallas_call x1, Pallas kernels, on_device_dense(): pl.pallas_call(block_kernel, out_shape=out, in_specs=[hbm] * 8, out_specs...  144 us

profile of v5, /device:TPU:0, one launch (start us, length us, event | category | flops | bytes accessed | tf_op | source)
XLA Modules:
  0.0 146.4 jit_solution(14644984725242230275)
XLA Ops:
  0.6 143.9 %shard_map.95 = f32[32,4096]{1,0:T(8,128)} custom-call(bf16[32,2048]{1,0:T(8,128)(2,1)} %tok_hbm.1, bf16[32,2048]{1,0:T(8,128)(2,1)} %tan_hbm.1, f32[1,2048]{1,0:T(1,128)} %bitcast.4, bf16[16,2048]{1,0:T(8,128)(2,1)} %bitcast.3, s32[8,32]{1,0:T(8,128)} %bitcast.5, bf16[2,512,768]{2,1,0:T(8,128)(2,1)} %wg_ref.1, bf16[2,512,768]{2,1,0:T(8,128)(2,1)} %wu_ref.1, ...), custom_call_target="tpu_custom_call" | custom-call | flops 12884901888 | bytes 16777216 | tf_op jit(solution)/shard_map/pallas_call | solution.py:632
  144.6 1.9 %fusion = (f32[32,2048]{1,0:T(8,128)}, f32[32,2048]{1,0:T(8,128)}) fusion(f32[32,4096]{1,0:T(8,128)} %shard_map.95), kind=kLoop, calls=%fused_computation | loop fusion | bytes 1048576 | tf_op jit(solution)/shard_map/slice | solution.py:671

commit v6 on v5

--- a/solution.py
+++ b/solution.py
@@ -573,15 +573,15 @@
     merge(0, 0, 3)
     merge(0, 0, 0)
     merge(0, 1, 2)
+    image_of(0)
     merge(0, 1, 1)
-    image_of(0)
     merge(0, 1, 3)
+    image_on(0, 0)
     merge(0, 1, 0)
-    image_on(0, 0)
+    image_of(1)
     image_on(0, 1)
-    image_of(1)
+    image_on(1, 0)
     image_on(0, 2)
-    image_on(1, 0)
     image_on(1, 1)
     image_on(1, 2)
     backward(0, 0)

time: 147 us -> 144 us (0.980)
  Pallas kernels: 144 us -> 142 us
    pallas_call x1, Pallas kernels: 144 us -> 142 us  [on_device_dense(): pl.pallas_call(block_kernel, out_shape=out, in_specs=[hbm] * 8, out_specs...]
where the time goes in v6:
time: 144 us
  Pallas kernels  142 us (99%)
  local copies, waits for them, and re-layouts  1.86 us (1%)
    pallas_call x1, Pallas kernels, on_device_dense(): pl.pallas_call(block_kernel, out_shape=out, in_specs=[hbm] * 8, out_specs...  142 us

profile of v6, /device:TPU:0, one launch (start us, length us, event | category | flops | bytes accessed | tf_op | source)
XLA Modules:
  0.0 144.2 jit_solution(3403671456316601649)
XLA Ops:
  0.6 141.7 %shard_map.95 = f32[32,4096]{1,0:T(8,128)} custom-call(bf16[32,2048]{1,0:T(8,128)(2,1)} %tok_hbm.1, bf16[32,2048]{1,0:T(8,128)(2,1)} %tan_hbm.1, f32[1,2048]{1,0:T(1,128)} %bitcast.4, bf16[16,2048]{1,0:T(8,128)(2,1)} %bitcast.3, s32[8,32]{1,0:T(8,128)} %bitcast.5, bf16[2,512,768]{2,1,0:T(8,128)(2,1)} %wg_ref.1, bf16[2,512,768]{2,1,0:T(8,128)(2,1)} %wu_ref.1, ...), custom_call_target="tpu_custom_call" | custom-call | flops 12884901888 | bytes 16777216 | tf_op jit(solution)/shard_map/pallas_call | solution.py:632
  142.4 1.9 %fusion = (f32[32,2048]{1,0:T(8,128)}, f32[32,2048]{1,0:T(8,128)}) fusion(f32[32,4096]{1,0:T(8,128)} %shard_map.95), kind=kLoop, calls=%fused_computation | loop fusion | bytes 1048576 | tf_op jit(solution)/shard_map/slice | solution.py:671

commit v7 on v6

--- a/solution.py
+++ b/solution.py
@@ -436,7 +436,12 @@
     turns = [
         (part, own_part, mid, far, landed), (part2, own_part2, mid2, far2, landed2)
     ]
-    x_copies, y_copies, z_copies, totals = {}, {}, {}, {}
+    x_copies, y_copies = {}, {}
+
+    def by_z(a, b, c, d):
+        return jnp.where(z < 2, jnp.where(z < 1, a, b), jnp.where(z < 3, c, d))
+
+    far_first = {0: 0, 2: by_z(3, 2, 2, 1), 1: by_z(2, 1, 3, 2), 3: by_z(1, 3, 1, 3)}
 
     def place(turn, b, l, cols, term):
         parts, own = turns[turn][0:2]
@@ -451,31 +456,38 @@
         parts, far = turns[turn][0], turns[turn][3]
         peer, base = ((x_peer, at_x), (y_peer, at_y))[s]
         copies = (x_copies, y_copies)[s]
-        for dz in (2, 1, 3, 0):
-            copies[turn, b, dz] = push(
+        for turn_no in (2, 1, 3, 0):
+            dz = far_first[turn_no]
+            copies[turn, b, turn_no] = push(
                 parts.at[b, rows_of(base, dz)], far.at[b, s, rows_of(0, dz)],
                 s_sems, (turn, b, s, dz), peer,
             )
 
-    def merge(turn, b, dz):
+    def merge(turn, b, turn_no):
         parts, own, mid, far, land = turns[turn]
-        x_copies[turn, b, dz].wait_recv()
-        y_copies[turn, b, dz].wait_recv()
+        dz = far_first[turn_no]
+        x_copies[turn, b, turn_no].wait_recv()
+        y_copies[turn, b, turn_no].wait_recv()
         at = rows_of(0, dz)
         total = own[b, at, :] + (far[b, 0, at, :].astype(f32) + far[b, 1, at, :].astype(f32))
-        if dz:
-            mid[b, dz] = total.astype(bf)
-            z_copies[turn, b, dz] = push(
-                mid.at[b, dz], land.at[b, z], z_sems, (turn, b, dz), z_peers[dz - 1]
+        if turn_no:
+            mid[b, turn_no] = total.astype(bf)
+            push(
+                mid.at[b, turn_no], land.at[b, z], z_sems, (turn, b, dz),
+                (dp, (z + dz) % 4 * 2 + core),
             )
         else:
             own[b, at, :] = total
 
     def total_of(turn, b):
-        own, land = turns[turn][1], turns[turn][4]
+        own, mid, land = turns[turn][1], turns[turn][2], turns[turn][4]
         total = own[b, rows_of(0, 0), :]
         for dz in (1, 3, 2):
-            z_copies[turn, b, dz].wait_recv()
+            pltpu.make_async_remote_copy(
+                src_ref=mid.at[b, dz], dst_ref=land.at[b, (z + 4 - dz) % 4],
+                send_sem=z_send.at[turn, b, dz], recv_sem=z_recv.at[turn, b, dz],
+                device_id=z_peers[dz - 1], device_id_type=MESH,
+            ).wait_recv()
             total = total + land[b, (z + 4 - dz) % 4].astype(f32)
         return total
 

time: 144 us -> 144 us (level)
  no operation moved by 1% of the time
where the time goes in v7:
time: 144 us
  Pallas kernels  141 us (98%)
  local copies, waits for them, and re-layouts  1.86 us (1%)
    pallas_call x1, Pallas kernels, on_device_dense(): pl.pallas_call(block_kernel, out_shape=out, in_specs=[hbm] * 8, out_specs...  141 us

profile of v7, /device:TPU:0, one launch (start us, length us, event | category | flops | bytes accessed | tf_op | source)
XLA Modules:
  0.0 143.5 jit_solution(16220677270872380364)
XLA Ops:
  0.6 141.0 %shard_map.95 = f32[32,4096]{1,0:T(8,128)} custom-call(bf16[32,2048]{1,0:T(8,128)(2,1)} %tok_hbm.1, bf16[32,2048]{1,0:T(8,128)(2,1)} %tan_hbm.1, f32[1,2048]{1,0:T(1,128)} %bitcast.4, bf16[16,2048]{1,0:T(8,128)(2,1)} %bitcast.3, s32[8,32]{1,0:T(8,128)} %bitcast.5, bf16[2,512,768]{2,1,0:T(8,128)(2,1)} %wg_ref.1, bf16[2,512,768]{2,1,0:T(8,128)(2,1)} %wu_ref.1, ...), custom_call_target="tpu_custom_call" | custom-call | flops 12884901888 | bytes 16777216 | tf_op jit(solution)/shard_map/pallas_call | solution.py:644
  141.7 1.9 %fusion = (f32[32,2048]{1,0:T(8,128)}, f32[32,2048]{1,0:T(8,128)}) fusion(f32[32,4096]{1,0:T(8,128)} %shard_map.95), kind=kLoop, calls=%fused_computation | loop fusion | bytes 1048576 | tf_op jit(solution)/shard_map/slice | solution.py:683

commit v8 on v7

--- a/solution.py
+++ b/solution.py
@@ -607,8 +607,8 @@
     merge(1, 1, 2)
     merge(1, 1, 1)
     merge(1, 1, 3)
+    gram_of(0)
     merge(1, 1, 0)
-    gram_of(0)
     gram_of(1)
     for copy in stores:
         copy.wait()

time: 144 us -> 144 us (level)
  no operation moved by 1% of the time
where the time goes in v8:
time: 144 us
  Pallas kernels  141 us (98%)
  local copies, waits for them, and re-layouts  1.86 us (1%)
    pallas_call x1, Pallas kernels, on_device_dense(): pl.pallas_call(block_kernel, out_shape=out, in_specs=[hbm] * 8, out_specs...  141 us

profile of v8, /device:TPU:0, one launch (start us, length us, event | category | flops | bytes accessed | tf_op | source)
XLA Modules:
  0.0 143.5 jit_solution(14376325755396626615)
XLA Ops:
  0.6 141.0 %shard_map.95 = f32[32,4096]{1,0:T(8,128)} custom-call(bf16[32,2048]{1,0:T(8,128)(2,1)} %tok_hbm.1, bf16[32,2048]{1,0:T(8,128)(2,1)} %tan_hbm.1, f32[1,2048]{1,0:T(1,128)} %bitcast.4, bf16[16,2048]{1,0:T(8,128)(2,1)} %bitcast.3, s32[8,32]{1,0:T(8,128)} %bitcast.5, bf16[2,512,768]{2,1,0:T(8,128)(2,1)} %wg_ref.1, bf16[2,512,768]{2,1,0:T(8,128)(2,1)} %wu_ref.1, ...), custom_call_target="tpu_custom_call" | custom-call | flops 12884901888 | bytes 16777216 | tf_op jit(solution)/shard_map/pallas_call | solution.py:644
  141.7 1.9 %fusion = (f32[32,2048]{1,0:T(8,128)}, f32[32,2048]{1,0:T(8,128)}) fusion(f32[32,4096]{1,0:T(8,128)} %shard_map.95), kind=kLoop, calls=%fused_computation | loop fusion | bytes 1048576 | tf_op jit(solution)/shard_map/slice | solution.py:683
